TPU v7x, 512 devices: a whole 4x4x16 slice. The times are simulated.
512 devices in a mesh: fib: 32 (over z_lo, x, core), oth: 16 (over z_hi, y).
Axes of the slice: x: 4, y: 4, z: 16 (z_hi: 4, z_lo: 4; z = z_hi * 4 + z_lo), core: 2. Of those that a mesh axis runs over, the one named last changes fastest.
Arguments:
- slab: float32 [1024, 16, 32, 128], P('fib', 'oth')
- start_basis: bfloat16 [1024, 128], replicated, may hold values from -6 to 6
Outputs:
- core: float32 [128, 16, 32, 128], P(None, 'oth', 'fib')
All inputs are finite; a program needn't handle non-finite values.
Results may differ from a plain program's by a relative error of at most 0.0023.
Values may be sent and summed in bfloat16 or wider, within the bound.
A program may use at most 64 MiB of HBM per device.

v0:
```python
import jax
import jax.numpy as jnp
from jax import lax
from jax.sharding import PartitionSpec as P

ITERS = 3


def orthonormal(image):
    square = jnp.dot(image.T, image, precision=lax.Precision.HIGHEST)
    low = jnp.linalg.cholesky(square)
    return lax.linalg.triangular_solve(low, image, left_side=False, lower=True, transpose_a=True)


def row_products(left, right):
    return lax.dot_general(
        left, right, (((1,), (1,)), ((), ())), preferred_element_type=jnp.float32
    )


def local(slab, start_basis):
    narrow_slab = slab.astype(jnp.bfloat16)
    moved = lax.all_to_all(narrow_slab, "fib", split_axis=2, concat_axis=0, tiled=True)
    fibres = moved.reshape(moved.shape[0], moved.shape[1] * moved.shape[2] * moved.shape[3])
    basis = start_basis.astype(jnp.float32)
    gram = lax.psum(row_products(fibres, fibres), ("fib", "oth"))
    for step in range(ITERS):
        image = jnp.dot(gram, basis, precision=lax.Precision.HIGHEST)
        basis = orthonormal(image)
    narrow = basis.astype(jnp.bfloat16)
    core = lax.dot_general(
        narrow, fibres, (((0,), (0,)), ((), ())), preferred_element_type=jnp.float32
    )
    return core.reshape(core.shape[0], 1, 1, core.shape[1])


def solution(mesh):
    placed = (P("fib", "oth", None, None), P())
    return jax.shard_map(
        local, mesh=mesh, in_specs=placed, out_specs=P(None, "oth", "fib", None), check_vma=False
    )
```

profile of v0, /device:TPU:1, one launch (start us, length us, event | category | flops | bytes accessed | tf_op | source)
XLA Modules:
  0.0 616.0 jit_solution(3177355466779141188)
XLA Ops:
  6.5 0.0 copy-start
  6.5 0.0 all-reduce.2.cloned.1.call-start
  6.5 1.4 copy.18
  7.9 20.9 %all_to_all.15 = bf16[32,1,32,128]{3,0,1,2:T(8,128)(2,1)S(1)} all-to-all(bf16[32,1,32,128]{3,0,1,2:T(8,128)(2,1)S(1)} %copy.18), channel_id=1, replica_groups=mesh['fib'=32,'oth'=16] {'fib'}, dimensions={2} | all-to-all | bytes 524288 | tf_op jit(solution)/shard_map/all_to_all | solution.py:23
  28.9 2.7 fusion.14
  31.5 0.0 all-reduce.2.cloned.1.call-update
  31.6 487.8 %all-reduce.2.cloned.1.call-done = f32[1024,1024]{1,0:T(8,128)} async-done(((f32[1024,1024]{1,0:T(8,128)}), f32[1024,1024]{1,0:T(8,128)}) %all-reduce.2.cloned.1.call-update) | async-done | bytes 4194320 | tf_op jit(solution)/shard_map/psum | solution.py:26
  519.4 0.0 copy-done
  519.4 4.1 fusion.15
  523.5 1.0 fusion.16
  524.6 0.1 copy.13
  524.7 11.7 %cholesky.59 = f32[128,128]{1,0:T(8,128)S(1)} custom-call(f32[128,128]{1,0:T(8,128)S(1)} %fusion.9), custom_call_target="Cholesky" | custom-call | tf_op jit(solution)/shard_map/jit(cholesky)/cholesky | solution.py:11
  536.4 0.6 compare_reduce_fusion.2
  537.1 0.7 fusion.1
  537.7 9.8 %custom-call.7 = f32[1,128,128]{1,2,0:T(8,128)S(1)} custom-call(f32[1,128,128]{2,1,0:T(8,128)S(1)} %fusion.1), custom_call_target="InvertDiagBlocksLowerTriangular" | custom-call | tf_op jit(solution)/shard_map/triangular_solve/custom-call.0 | solution.py:12
  547.5 0.6 convolution_bitcast_fusion.2
  548.2 5.4 fusion.17
  553.6 1.0 fusion.18
  554.6 0.1 copy.14
  554.7 11.7 %cholesky.70 = f32[128,128]{1,0:T(8,128)S(1)} custom-call(f32[128,128]{1,0:T(8,128)S(1)} %fusion.7), custom_call_target="Cholesky" | custom-call | tf_op jit(solution)/shard_map/jit(cholesky)/cholesky | solution.py:11
  566.5 0.6 compare_reduce_fusion.1
  567.1 0.7 fusion.2
  567.8 9.8 %custom-call.8 = f32[1,128,128]{1,2,0:T(8,128)S(1)} custom-call(f32[1,128,128]{2,1,0:T(8,128)S(1)} %fusion.2), custom_call_target="InvertDiagBlocksLowerTriangular" | custom-call | tf_op jit(solution)/shard_map/triangular_solve/custom-call.0 | solution.py:12
  577.6 0.6 convolution_bitcast_fusion.1
  578.2 5.4 fusion.19
  583.7 1.0 fusion.20
  584.7 0.1 copy.15
  584.8 11.7 %cholesky.81 = f32[128,128]{1,0:T(8,128)S(1)} custom-call(f32[128,128]{1,0:T(8,128)S(1)} %fusion.5), custom_call_target="Cholesky" | custom-call | tf_op jit(solution)/shard_map/jit(cholesky)/cholesky | solution.py:11
  596.6 0.6 compare_reduce_fusion
  597.2 0.7 fusion.3
  597.9 9.8 %custom-call.9 = f32[1,128,128]{1,2,0:T(8,128)S(1)} custom-call(f32[1,128,128]{2,1,0:T(8,128)S(1)} %fusion.3), custom_call_target="InvertDiagBlocksLowerTriangular" | custom-call | tf_op jit(solution)/shard_map/triangular_solve/custom-call.0 | solution.py:12
  607.7 0.6 fusion
  608.3 0.9 fusion.21
  (6 shorter events, 0.1 us)
Async XLA Ops:
  6.5 512.9 %copy-start = (bf16[1024,128]{1,0:T(8,128)(2,1)S(1)}, bf16[1024,128]{1,0:T(8,128)(2,1)}, u32[]{:S(2)}) copy-start(bf16[1024,128]{1,0:T(8,128)(2,1)} %param.6) | copy-start | bytes 786436
  6.5 512.9 %all-reduce.2.cloned.1.call-start = ((), (), s32[]{:S(2)}) async-start(), calls=%async_computation.1 | async-start | bytes 8388608 | tf_op jit(solution)/shard_map/psum | solution.py:26
Sparse Core Ops, SparseCore 0:
  31.7 487.6 all-reduce.1
where the time goes:
time: 618 us; the launch traced here: 616 us
  waiting for transfers between devices  488 us (79%)
  other arithmetic  68.6 us (11%)
  matrix products  23.5 us (4%)
  blocking collectives  20.9 us (3%)
  between operations  13.5 us (2%)
    psum x1, waiting for transfers between devices, local(): gram = lax.psum(row_products(fibres, fibres), ('fib', 'oth'))  488 us
    another operation x9, other arithmetic, orthonormal(): low = jnp.linalg.cholesky(square)  37.2 us
    another operation x6, other arithmetic, orthonormal(): lax.linalg.triangular_solve(low, image, left_side=False, lower=True, tran...  31.4 us
    all_to_all x1, blocking collectives, local(): lax.all_to_all(narrow_slab, 'fib', split_axis=2, concat_axis=0, tiled=True)  20.9 us
    dot_general x3, matrix products, local(): image = jnp.dot(gram, basis, precision=lax.Precision.HIGHEST)  15 us
  transfers between devices with their start and end apart: 1, of which 1 were waited for; matrix products, arithmetic and copies ran while one was open for 0% of the time, Pallas kernels for 0%

commit v1 on v0

v1 whole, which is shorter than its diff:
```python
import functools

import jax
import jax.numpy as jnp
from jax import lax
from jax.experimental import pallas as pl
from jax.experimental.pallas import tpu as pltpu
from jax.sharding import PartitionSpec as P

ITERS = 3
RANK = 128
CELLS = 128
CHUNK = 8
GRID = dict(zl=4, x=4, c=2, zh=4, y=4)
MESH = pl.DeviceIdType.MESH
F32 = jnp.float32
BF16 = jnp.bfloat16


def thirds(a):
    high = a.astype(BF16)
    rest = a - high.astype(F32)
    mid = rest.astype(BF16)
    return high, mid, (rest - mid.astype(F32)).astype(BF16)


def sublane(v, s):
    return jnp.broadcast_to(v[s : s + 1, :], v.shape)


def panel_step(b, work, inverse):
    base = pl.multiple_of(b * 8, 8)
    left = work[pl.ds(base, 8), 0:RANK]
    right = work[pl.ds(base, 8), RANK : 2 * RANK]
    turned = pltpu.roll(left, RANK - base, 1)
    cols = [jnp.broadcast_to(turned[:, s : s + 1], (8, RANK)) for s in range(8)]
    row = lax.broadcasted_iota(jnp.int32, (8, RANK), 0)
    lane = lax.broadcasted_iota(jnp.int32, (8, RANK), 1)
    pivots = jnp.zeros((8, RANK), F32)
    for s in range(8):
        pivot = sublane(cols[s], s)
        pivots = jnp.where(row == s, pivot, pivots)
        if s < 7:
            factor = jnp.where(row > s, cols[s] * (1.0 / pivot), 0.0)
            for u in range(s + 1, 8):
                cols[u] = cols[u] - factor * sublane(cols[u], s)
            left = left - factor * sublane(left, s)
            right = right - factor * sublane(right, s)
    inverse[pl.ds(base, 8), :] = right * lax.rsqrt(pivots)
    factors = jnp.where(lane >= base + 8, left * (1.0 / pivots), 0.0)
    fh, fm, fl = [t.astype(F32) for t in thirds(factors)]
    rh, rm, rl = [t.astype(F32) for t in thirds(jnp.concatenate([left, right], axis=1))]
    tall = jnp.concatenate([fh, fh, fm, fh, fl, fm], axis=0).astype(BF16)
    wide = jnp.concatenate([rh, rm, rh, rl, rh, rm], axis=0).astype(BF16)
    work[...] = work[...] - lax.dot_general(
        tall, wide, (((0,), (0,)), ((), ())), preferred_element_type=F32
    )


def start_factor(image, work):
    work[:, 0:RANK] = lax.dot_general(
        image, image, (((0,), (0,)), ((), ())),
        preferred_element_type=F32, precision=lax.Precision.HIGHEST,
    )
    i0 = lax.broadcasted_iota(jnp.int32, (RANK, RANK), 0)
    i1 = lax.broadcasted_iota(jnp.int32, (RANK, RANK), 1)
    work[:, RANK : 2 * RANK] = (i0 == i1).astype(F32)


def to_unit(image):
    return image * (1.0 / jnp.max(jnp.abs(image)))


def kernel(
    grid, slab, start, out,
    stage, send, flat, part, from_core, summed, from_y, chunks, from_zl, from_zh, own, mine,
    image, images, work, inverse,
    load_sem, a_send, a_recv, x_send, x_recv, c_send, c_recv, y_send, y_recv,
    zl_send, zl_recv, zh_send, zh_recv, g_send, g_recv, p_send, p_recv, local_sem,
):
    nzl, nx, nc, nzh, ny = (grid[k] for k in ("zl", "x", "c", "zh", "y"))
    rows = stage.shape[1]
    fib, oth = lax.axis_index("fib"), lax.axis_index("oth")
    c = lax.rem(fib, nc)
    x = lax.rem(lax.div(fib, nc), nx)
    zl = lax.div(fib, nc * nx)
    y = lax.rem(oth, ny)
    zh = lax.div(oth, ny)

    def device(dzl=0, dx=0, dc=0, dzh=0, dy=0):
        f = (lax.rem(zl + dzl, nzl) * nx + lax.rem(x + dx, nx)) * nc + lax.rem(c + dc, nc)
        o = lax.rem(zh + dzh, nzh) * ny + lax.rem(y + dy, ny)
        return (f, o)

    def copy(src, dst, ssem, rsem, to):
        return pltpu.make_async_remote_copy(
            src_ref=src, dst_ref=dst, send_sem=ssem, recv_sem=rsem,
            device_id=to, device_id_type=MESH,
        )

    run = [(dz, dc) for dz in range(nzl) for dc in range(nc) if dz or dc]
    plane = [(dx, dy) for dx in range(nx) for dy in range(ny) if dx or dy]

    loads = []
    for dz in range(nzl):
        to_zl = lax.rem(zl + dz, nzl)
        load = pltpu.make_async_copy(slab.at[:, to_zl], stage.at[dz], load_sem.at[dz])
        load.start()
        loads.append(load)

    barrier = pltpu.get_barrier_semaphore()
    peers = [device(dzh=k) for k in range(1, nzh)]
    peers += [device(dzl=dz, dc=dc) for dz, dc in run]
    peers += [device(dx=dx, dy=dy) for dx, dy in plane]
    for peer in peers:
        pl.semaphore_signal(barrier, inc=1, device_id=peer, device_id_type=MESH)

    for dz in range(nzl):
        loads[dz].wait()
        for px in range(nx):
            v0 = stage[dz, :, px * nc, :]
            v1 = stage[dz, :, px * nc + 1, :]
            same = jnp.where(c == 0, v0, v1).astype(BF16)
            other = jnp.where(c == 0, v1, v0).astype(BF16)
            send[dz, 0, :, px * CELLS : (px + 1) * CELLS] = same
            send[dz, 1, :, px * CELLS : (px + 1) * CELLS] = other

    pl.semaphore_wait(barrier, len(peers))

    started = []
    here = flat.at[pl.ds(pl.multiple_of(fib * rows, rows), rows), :]
    keep = pltpu.make_async_copy(send.at[0, 0], here, local_sem)
    keep.start()
    first = []
    for dz, dc in reversed(run):
        cp = copy(send.at[dz, dc], here, a_send.at[dz, dc], a_recv.at[dz, dc], device(dzl=dz, dc=dc))
        cp.start()
        first.append(cp)
    forwards = []

    def forward(dz, dc, src):
        block = (lax.rem(zl + nzl - dz, nzl) * nx + x) * nc + lax.rem(c + nc - dc, nc)
        dst = flat.at[pl.ds(pl.multiple_of(block * rows, rows), rows), :]
        for dx in range(1, nx):
            cp = copy(
                dst if src is None else src, dst,
                x_send.at[dx, dz, dc], x_recv.at[dx, dz, dc], device(dx=dx),
            )
            cp.start()
            forwards.append(cp)

    forward(0, 0, send.at[0, 0])
    keep.wait()
    for (dz, dc), cp in zip(run, reversed(first)):
        cp.wait_recv()
        forward(dz, dc, None)
    for cp in forwards:
        cp.wait_recv()
    started += first + forwards

    tops = [
        flat[pl.ds(pl.multiple_of((q * nx + x) * nc * rows, nc * rows), nc * rows), :]
        for q in range(nzl)
    ]
    gram = lax.dot_general(
        jnp.concatenate(tops, axis=0), flat[...], (((1,), (1,)), ((), ())),
        preferred_element_type=F32,
    )
    part[...] = gram.reshape(part.shape)
    sends = []
    for q in range(ny):
        cp = copy(part.at[q, 1 - c], from_core.at[q], c_send.at[q], c_recv.at[q], device(dc=1))
        cp.start()
        sends.append(cp)
    for cp in sends:
        cp.wait_recv()
    started += sends
    for q in range(ny):
        summed[q] = part[q, c] + from_core[q]
    sends = []
    for d in range(1, ny):
        cp = copy(summed.at[lax.rem(y + d, ny)], from_y.at[y], y_send.at[d], y_recv.at[d], device(dy=d))
        cp.start()
        sends.append(cp)
    from_y[y] = summed[y]
    for cp in sends:
        cp.wait_recv()
    started += sends
    total = from_y[0]
    for q in range(1, ny):
        total = total + from_y[q]
    chunks[...] = total.reshape(chunks.shape)
    sends = []
    for d in range(1, nzl):
        cp = copy(chunks.at[lax.rem(zl + d, nzl)], from_zl.at[zl], zl_send.at[d], zl_recv.at[d], device(dzl=d))
        cp.start()
        sends.append(cp)
    from_zl[zl] = chunks[zl]
    for cp in sends:
        cp.wait_recv()
    started += sends
    total = from_zl[0]
    for q in range(1, nzl):
        total = total + from_zl[q]
    from_zh[zh] = total
    sends = []
    for d in range(1, nzh):
        cp = copy(from_zh.at[zh], from_zh.at[zh], zh_send.at[d], zh_recv.at[d], device(dzh=d))
        cp.start()
        sends.append(cp)
    for cp in sends:
        cp.wait_recv()
    started += sends
    total = from_zh[0]
    for q in range(1, nzh):
        total = total + from_zh[q]
    own[...] = total

    chip = (y * nx + x) * nc * nzl
    tile = chip + c * nzl + zl

    def gather_start(k, value):
        mine[k] = value
        images[k, pl.ds(pl.multiple_of(tile * CHUNK, CHUNK), CHUNK), :] = value
        dst = images.at[k, pl.ds(pl.multiple_of(tile * CHUNK, CHUNK), CHUNK), :]
        cps = []
        for dz, dc in run:
            cp = copy(mine.at[k], dst, g_send.at[k, dz, dc], g_recv.at[k, dz, dc], device(dzl=dz, dc=dc))
            cp.start()
            cps.append(cp)
        return cps

    def gather_spread(k, cps):
        for cp in cps:
            cp.wait_recv()
        size = nc * nzl * CHUNK
        block = images.at[k, pl.ds(pl.multiple_of(chip * CHUNK, size), size), :]
        more = []
        for dx, dy in plane:
            cp = copy(block, block, p_send.at[k, dx, dy], p_recv.at[k, dx, dy], device(dx=dx, dy=dy))
            cp.start()
            more.append(cp)
        return cps, more

    def gather_end(cps, more):
        for cp in more:
            cp.wait_recv()
        for cp in cps + more:
            cp.wait_send()

    cps = gather_start(0, jnp.dot(own[...], start[...].astype(F32), preferred_element_type=F32,
                                  precision=lax.Precision.HIGHEST))
    for cp in started:
        cp.wait_send()
    gather_end(*gather_spread(0, cps))
    image[...] = to_unit(images[0])
    for k in range(1, ITERS):
        cps = gather_start(k, jnp.dot(own[...], image[...], preferred_element_type=F32,
                                      precision=lax.Precision.HIGHEST))
        start_factor(image[...], work)
        lax.fori_loop(0, 2, lambda b, _: (panel_step(b, work, inverse), 0)[1], 0)
        both = gather_spread(k, cps)
        lax.fori_loop(2, RANK // 8, lambda b, _: (panel_step(b, work, inverse), 0)[1], 0)
        gather_end(*both)
        image[...] = to_unit(lax.dot_general(
            images[k], inverse[...], (((1,), (1,)), ((), ())),
            preferred_element_type=F32, precision=lax.Precision.HIGHEST,
        ))
    start_factor(image[...], work)
    lax.fori_loop(0, RANK // 8, lambda b, _: (panel_step(b, work, inverse), 0)[1], 0)
    narrow = lax.dot_general(
        image[...], inverse[...], (((1,), (1,)), ((), ())),
        preferred_element_type=F32, precision=lax.Precision.HIGHEST,
    ).astype(BF16)
    out[...] = lax.dot_general(
        narrow, flat[:, pl.ds(pl.multiple_of(x * CELLS, CELLS), CELLS)],
        (((0,), (0,)), ((), ())), preferred_element_type=F32,
    )


def local(grid, slab, start):
    nzl, nx, nc, nzh, ny = (grid[k] for k in ("zl", "x", "c", "zh", "y"))
    rows = slab.shape[0]
    order = start.shape[0]
    wide = nx * CELLS
    dma = pltpu.SemaphoreType.DMA
    core = pl.pallas_call(
        functools.partial(kernel, grid),
        out_shape=jax.ShapeDtypeStruct((RANK, CELLS), F32),
        in_specs=[pl.BlockSpec(memory_space=pl.ANY), pl.BlockSpec(memory_space=pltpu.VMEM)],
        out_specs=pl.BlockSpec(memory_space=pltpu.VMEM),
        scratch_shapes=[
            pltpu.VMEM((nzl, rows, nx * nc, CELLS), F32),
            pltpu.VMEM((nzl, nc, rows, wide), BF16),
            pltpu.VMEM((order, wide), BF16),
            pltpu.VMEM((ny, nc, rows, order), F32),
            pltpu.VMEM((ny, rows, order), F32),
            pltpu.VMEM((ny, rows, order), F32),
            pltpu.VMEM((ny, rows, order), F32),
            pltpu.VMEM((nzl, CHUNK, order), F32),
            pltpu.VMEM((nzl, CHUNK, order), F32),
            pltpu.VMEM((nzh, CHUNK, order), F32),
            pltpu.VMEM((CHUNK, order), F32),
            pltpu.VMEM((ITERS, CHUNK, RANK), F32),
            pltpu.VMEM((order, RANK), F32),
            pltpu.VMEM((ITERS, order, RANK), F32),
            pltpu.VMEM((RANK, 2 * RANK), F32),
            pltpu.VMEM((RANK, RANK), F32),
            dma((nzl,)),
            dma((nzl, nc)), dma((nzl, nc)),
            dma((nx, nzl, nc)), dma((nx, nzl, nc)),
            dma((ny,)), dma((ny,)),
            dma((ny,)), dma((ny,)),
            dma((nzl,)), dma((nzl,)),
            dma((nzh,)), dma((nzh,)),
            dma((ITERS, nzl, nc)), dma((ITERS, nzl, nc)),
            dma((ITERS, nx, ny)), dma((ITERS, nx, ny)),
            dma(()),
        ],
        compiler_params=pltpu.CompilerParams(
            collective_id=0, has_side_effects=True, vmem_limit_bytes=40 * 2**20
        ),
        name="truncate",
    )(slab.reshape(rows, nzl, nx * nc, CELLS), start)
    return core.reshape(RANK, 1, 1, CELLS)


def solution(mesh, grid=GRID):
    placed = (P("fib", "oth", None, None), P())
    return jax.shard_map(
        functools.partial(local, grid), mesh=mesh, in_specs=placed,
        out_specs=P(None, "oth", "fib", None), check_vma=False,
    )
```

time: 618 us -> 112 us (0.18)
  waiting for transfers between devices: 488 us -> 0 us
  Pallas kernels: 0 us -> 109 us
  other arithmetic: 68.6 us -> 0 us
  matrix products: 23.5 us -> 0 us
  blocking collectives: 20.9 us -> 0 us
  between operations: 13.5 us -> 0.01 us
    psum x1 -> x0, waiting for transfers between devices: 488 us -> none  [local(): gram = lax.psum(row_products(fibres, fibres), ('fib', 'oth'))]
    pallas_call x0 -> x1, Pallas kernels: none -> 109 us  [local(): pl.pallas_call(functools.partial(kernel, grid), out_shape=jax.ShapeDtypeS...]
    another operation x15 -> x0, other arithmetic: 68.6 us -> none  [the longest x9 37.2 us: orthonormal(): low = jnp.linalg.cholesky(square)]
    dot_general x8 -> x0, matrix products: 21.5 us -> none  [the longest x3 15 us: local(): image = jnp.dot(gram, basis, precision=lax.Precision.HIGHEST)]
    all_to_all x1 -> x0, blocking collectives: 20.9 us -> none  [local(): lax.all_to_all(narrow_slab, 'fib', split_axis=2, concat_axis=0, tiled=True)]
  transfers between devices with their start and end apart: 1 -> 0, of which waited for: 1 -> 0; matrix products, arithmetic and copies ran while one was open for 0% -> 0% of each run, Pallas kernels for 0% -> 0%
where the time goes in v1:
time: 112 us
  Pallas kernels  109 us (97%)
  local copies, waits for them, and re-layouts  2.62 us (2%)
    pallas_call x1, Pallas kernels, local(): pl.pallas_call(functools.partial(kernel, grid), out_shape=jax.ShapeDtypeS...  109 us
    unnamed x5, local copies, waits for them, and re-layouts  2.62 us

profile of v1, /device:TPU:1, one launch (start us, length us, event | category | flops | bytes accessed | tf_op | source)
XLA Modules:
  0.0 111.9 jit_solution(10683698027373144241)
XLA Ops:
  0.0 0.0 copy-start
  0.0 1.0 copy-done
  1.0 0.0 copy-start.1
  1.0 0.9 copy-done.1
  2.0 109.3 %truncate.1 = f32[128,128]{1,0:T(8,128)S(1)} custom-call(f32[32,4,8,128]{3,2,1,0:T(8,128)S(1)} %bitcast.4, bf16[1024,128]{1,0:T(8,128)(2,1)S(1)} %copy-done.1), custom_call_target="tpu_custom_call" | custom-call | tf_op jit(solution)/shard_map/truncate/pallas_call | solution.py:287
  111.3 0.6 copy.5
Async XLA Ops:
  0.0 1.0 copy-start
  1.0 0.9 copy-start.1

commit v2 on v1

v2 whole, which is shorter than its diff:
```python
import functools

import jax
import jax.numpy as jnp
from jax import lax
from jax.experimental import pallas as pl
from jax.experimental.pallas import tpu as pltpu
from jax.sharding import PartitionSpec as P

ITERS = 3
RANK = 128
CELLS = 128
CHUNK = 8
GRID = dict(zl=4, x=4, c=2, zh=4, y=4)
MESH = pl.DeviceIdType.MESH
F32 = jnp.float32
BF16 = jnp.bfloat16


def thirds(a):
    high = a.astype(BF16)
    rest = a - high.astype(F32)
    mid = rest.astype(BF16)
    return high, mid, (rest - mid.astype(F32)).astype(BF16)


def sublane(v, s):
    return jnp.broadcast_to(v[s : s + 1, :], v.shape)


def panel_step(b, work, inverse):
    base = pl.multiple_of(b * 8, 8)
    left = work[pl.ds(base, 8), 0:RANK]
    right = work[pl.ds(base, 8), RANK : 2 * RANK]
    turned = pltpu.roll(left, RANK - base, 1)
    cols = [jnp.broadcast_to(turned[:, s : s + 1], (8, RANK)) for s in range(8)]
    row = lax.broadcasted_iota(jnp.int32, (8, RANK), 0)
    lane = lax.broadcasted_iota(jnp.int32, (8, RANK), 1)
    pivots = jnp.zeros((8, RANK), F32)
    for s in range(8):
        pivot = sublane(cols[s], s)
        pivots = jnp.where(row == s, pivot, pivots)
        if s < 7:
            factor = jnp.where(row > s, cols[s] * (1.0 / pivot), 0.0)
            for u in range(s + 1, 8):
                cols[u] = cols[u] - factor * sublane(cols[u], s)
            left = left - factor * sublane(left, s)
            right = right - factor * sublane(right, s)
    inverse[pl.ds(base, 8), :] = right * lax.rsqrt(pivots)
    factors = jnp.where(lane >= base + 8, left * (1.0 / pivots), 0.0)
    fh, fm, fl = [t.astype(F32) for t in thirds(factors)]
    rh, rm, rl = [t.astype(F32) for t in thirds(jnp.concatenate([left, right], axis=1))]
    tall = jnp.concatenate([fh, fh, fm, fh, fl, fm], axis=0).astype(BF16)
    wide = jnp.concatenate([rh, rm, rh, rl, rh, rm], axis=0).astype(BF16)
    work[...] = work[...] - lax.dot_general(
        tall, wide, (((0,), (0,)), ((), ())), preferred_element_type=F32
    )


def start_factor(image, work):
    work[:, 0:RANK] = lax.dot_general(
        image, image, (((0,), (0,)), ((), ())),
        preferred_element_type=F32, precision=lax.Precision.HIGHEST,
    )
    i0 = lax.broadcasted_iota(jnp.int32, (RANK, RANK), 0)
    i1 = lax.broadcasted_iota(jnp.int32, (RANK, RANK), 1)
    work[:, RANK : 2 * RANK] = (i0 == i1).astype(F32)


def to_unit(image):
    return image * (1.0 / jnp.max(jnp.abs(image)))


def kernel(
    grid, slab, start, out,
    stage, basis, send, flat, part, from_core, summed, relay, from_y, chunks, from_zl, from_zh, own,
    small, s_core, s_summed, s_y, s_chunks, s_zl, s_zh,
    mine, image, images, work, inverse,
    load_sem, local_sem, a_send, a_recv, x_send, x_recv, c_send, c_recv, r_send, r_recv, y_send, y_recv,
    zl_send, zl_recv, zh_send, zh_recv, sc_send, sc_recv, sy_send, sy_recv, sl_send, sl_recv, sh_send, sh_recv,
    g_send, g_recv, p_send, p_recv, q_send, q_recv,
):
    nzl, nx, nc, nzh, ny = (grid[k] for k in ("zl", "x", "c", "zh", "y"))
    rows = stage.shape[1]
    deep = summed.shape[1]
    half = deep // 2
    fib, oth = lax.axis_index("fib"), lax.axis_index("oth")
    c = lax.rem(fib, nc)
    x = lax.rem(lax.div(fib, nc), nx)
    zl = lax.div(fib, nc * nx)
    y = lax.rem(oth, ny)
    zh = lax.div(oth, ny)

    def device(dzl=0, dx=0, dc=0, dzh=0, dy=0):
        f = (lax.rem(zl + dzl, nzl) * nx + lax.rem(x + dx, nx)) * nc + lax.rem(c + dc, nc)
        o = lax.rem(zh + dzh, nzh) * ny + lax.rem(y + dy, ny)
        return (f, o)

    started = []

    def copy(src, dst, ssem, rsem, to):
        cp = pltpu.make_async_remote_copy(
            src_ref=src, dst_ref=dst, send_sem=ssem, recv_sem=rsem,
            device_id=to, device_id_type=MESH,
        )
        cp.start()
        started.append(cp)
        return cp

    def landed(cps):
        for cp in cps:
            cp.wait_recv()

    run = [(dz, dc) for dz in range(nzl) for dc in range(nc)]
    plane = [(dx, dy) for dx in range(nx) for dy in range(ny) if dx or dy]

    loads = []
    for dz in range(nzl):
        to_zl = lax.rem(zl + dz, nzl)
        load = pltpu.make_async_copy(slab.at[:, to_zl], stage.at[dz], load_sem.at[dz])
        load.start()
        loads.append(load)
    load_basis = pltpu.make_async_copy(start, basis, load_sem.at[nzl])
    load_basis.start()

    barrier = pltpu.get_barrier_semaphore()
    peers = [device(dzh=k) for k in range(1, nzh)]
    peers += [device(dzl=dz, dc=dc) for dz, dc in run[1:]]
    peers += [device(dx=dx, dy=dy) for dx, dy in plane]
    for peer in peers:
        pl.semaphore_signal(barrier, inc=1, device_id=peer, device_id_type=MESH)

    for dz in range(nzl):
        loads[dz].wait()
        for px in range(nx):
            v0 = stage[dz, :, px * nc, :]
            v1 = stage[dz, :, px * nc + 1, :]
            same = jnp.where(c == 0, v0, v1).astype(BF16)
            other = jnp.where(c == 0, v1, v0).astype(BF16)
            send[dz, 0, :, px * CELLS : (px + 1) * CELLS] = same
            send[dz, 1, :, px * CELLS : (px + 1) * CELLS] = other

    pl.semaphore_wait(barrier, len(peers))

    def block(dx, dz, dc):
        b = (lax.rem(zl + nzl - dz, nzl) * nx + lax.rem(x + dx, nx)) * nc + lax.rem(c + nc - dc, nc)
        return flat.at[pl.ds(pl.multiple_of(b * rows, rows), rows), :]

    here = block(0, 0, 0)
    keep = pltpu.make_async_copy(send.at[0, 0], here, local_sem)
    keep.start()
    first = {}
    for dz, dc in run[:0:-1]:
        first[dz, dc] = copy(send.at[dz, dc], here, a_send.at[dz, dc], a_recv.at[dz, dc], device(dzl=dz, dc=dc))
    right, left, more = {}, {}, []

    def onward(p):
        landed([right[p], left[p]])
        if p[1] == 0:
            src = block(nx - 1, *p)
            more.append(copy(src, src, x_send.at[2, *p], x_recv.at[2, *p], device(dx=1)))
        else:
            src = block(1, *p)
            more.append(copy(src, src, x_send.at[2, *p], x_recv.at[2, *p], device(dx=nx - 1)))

    for n, p in enumerate(run):
        src = dst = block(0, *p)
        if n:
            landed([first[p]])
        else:
            src = send.at[0, 0]
        right[p] = copy(src, dst, x_send.at[0, *p], x_recv.at[0, *p], device(dx=1))
        left[p] = copy(src, dst, x_send.at[1, *p], x_recv.at[1, *p], device(dx=nx - 1))
        if n >= 4:
            onward(run[n - 4])
    for p in run[-4:]:
        onward(p)
    landed(more)
    keep.wait()
    load_basis.wait()

    tops = jnp.concatenate([
        flat[pl.ds(pl.multiple_of(((q * nx + x) * nc + k) * rows, rows), rows), :]
        for k in range(nc) for q in range(nzl)
    ], axis=0)
    inner = lax.dot_general(
        basis[...], flat[...], (((0,), (0,)), ((), ())), preferred_element_type=F32
    )
    first_image = sum(
        lax.dot_general(tops, t, (((1,), (1,)), ((), ())), preferred_element_type=F32)
        for t in thirds(inner)[::-1]
    )
    small[...] = first_image.reshape(small.shape)
    cp = copy(small.at[1 - c], s_core, sc_send, sc_recv, device(dc=1))
    landed([cp])
    s_summed[...] = small[c] + s_core[...]
    s_y[y] = s_summed[y]
    small_y = [
        copy(s_summed.at[lax.rem(y + d, ny)], s_y.at[y], sy_send.at[d], sy_recv.at[d], device(dy=d))
        for d in (2, 1, 3)
    ]

    gram = lax.dot_general(tops, flat[...], (((1,), (1,)), ((), ())), preferred_element_type=F32)
    part[...] = gram.reshape(part.shape)
    across = []
    for d in (2, 1, 3, 0):
        q = lax.rem(y + d, ny)
        across.append((q, copy(part.at[1 - c, q], from_core.at[q], c_send.at[d], c_recv.at[d], device(dc=1))))

    landed(small_y)
    s_chunks[...] = sum(s_y[q] for q in range(ny)).reshape(s_chunks.shape)
    s_zl[zl] = s_chunks[zl]
    small_zl = [
        copy(s_chunks.at[lax.rem(zl + d, nzl)], s_zl.at[zl], sl_send.at[d], sl_recv.at[d], device(dzl=d))
        for d in range(1, nzl)
    ]

    low, high = pl.ds(0, half), pl.ds(half, half)
    nxt, prv, far = (lax.rem(y + d, ny) for d in (1, 3, 2))
    for n, (q, cp) in enumerate(across):
        landed([cp])
        summed[q] = part[c, q] + from_core[q]
        if n == 0:
            up = copy(summed.at[far, low], relay.at[0], r_send.at[0], r_recv.at[0], device(dy=1))
            down = copy(summed.at[far, high], relay.at[1], r_send.at[1], r_recv.at[1], device(dy=3))
        if n == 1:
            direct_up = copy(summed.at[nxt, high], from_y.at[0, high], y_send.at[0], y_recv.at[0], device(dy=1))
        if n == 2:
            direct_down = copy(summed.at[prv, low], from_y.at[1, low], y_send.at[1], y_recv.at[1], device(dy=3))

    landed([up])
    summed[nxt, low] = summed[nxt, low] + relay[0]
    last_up = copy(summed.at[nxt, low], from_y.at[0, low], y_send.at[2], y_recv.at[2], device(dy=1))
    landed([down])
    summed[prv, high] = summed[prv, high] + relay[1]
    last_down = copy(summed.at[prv, high], from_y.at[1, high], y_send.at[3], y_recv.at[3], device(dy=3))
    landed(small_zl)
    s_zh[zh] = sum(s_zl[q] for q in range(nzl))
    small_zh = [
        copy(s_zh.at[zh], s_zh.at[zh], sh_send.at[d], sh_recv.at[d], device(dzh=d))
        for d in range(1, nzh)
    ]

    landed([direct_up, direct_down, last_up, last_down])
    chunks[...] = (summed[y] + (from_y[0] + from_y[1])).reshape(chunks.shape)
    from_zl[zl] = chunks[zl]
    big_zl = [
        copy(chunks.at[lax.rem(zl + d, nzl)], from_zl.at[zl], zl_send.at[d], zl_recv.at[d], device(dzl=d))
        for d in range(1, nzl)
    ]

    def place(dx, dy, core):
        rho = lax.rem(y + dy, ny) * deep
        b = (lax.div(rho, rows) * nx + lax.rem(x + dx, nx)) * nc + core
        return b * rows + lax.rem(rho, rows)

    line = nzl * CHUNK

    def block_of(k, dx, dy, core):
        return images.at[k, pl.ds(pl.multiple_of(place(dx, dy, core), line), line), :]

    def gather_start(k, value):
        mine[k] = value
        where = pl.ds(pl.multiple_of(place(0, 0, c) + zl * CHUNK, CHUNK), CHUNK)
        images[k, where, :] = value
        return [
            copy(mine.at[k], images.at[k, where, :], g_send.at[k, d], g_recv.at[k, d], device(dzl=d))
            for d in range(1, nzl)
        ]

    def gather_spread(k, cps):
        landed(cps)
        src = block_of(k, 0, 0, c)
        spread = {
            (dx, dy): copy(src, src, p_send.at[k, dx, dy], p_recv.at[k, dx, dy], device(dx=dx, dy=dy))
            for dx, dy in sorted(plane, key=lambda p: -min(p[0], nx - p[0]) - min(p[1], ny - p[1]))
        }
        return spread, [copy(src, src, q_send.at[k, 0, 0], q_recv.at[k, 0, 0], device(dc=1))]

    def gather_end(k, spread, last):
        for dx, dy in sorted(plane, key=lambda p: min(p[0], nx - p[0]) + min(p[1], ny - p[1])):
            landed([spread[dx, dy]])
            src = block_of(k, nx - dx, ny - dy, c)
            last.append(copy(src, src, q_send.at[k, dx, dy], q_recv.at[k, dx, dy], device(dc=1)))
        landed(last)

    def factor(k0, k1):
        lax.fori_loop(k0, k1, lambda b, _: (panel_step(b, work, inverse), 0)[1], 0)

    landed(small_zh)
    cps = gather_start(0, sum(s_zh[q] for q in range(nzh)))
    landed(big_zl)
    from_zh[zh] = sum(from_zl[q] for q in range(nzl))
    big_zh = [
        copy(from_zh.at[zh], from_zh.at[zh], zh_send.at[d], zh_recv.at[d], device(dzh=d))
        for d in range(1, nzh)
    ]
    gather_end(0, *gather_spread(0, cps))
    image[...] = to_unit(images[0])
    start_factor(image[...], work)
    landed(big_zh)
    own[...] = sum(from_zh[q] for q in range(nzh))
    for k in range(1, ITERS):
        cps = gather_start(k, jnp.dot(own[...], image[...], preferred_element_type=F32,
                                      precision=lax.Precision.HIGHEST))
        if k > 1:
            start_factor(image[...], work)
        factor(0, 4 if k == 1 else 2)
        both = gather_spread(k, cps)
        factor(4 if k == 1 else 2, RANK // 8)
        gather_end(k, *both)
        image[...] = to_unit(lax.dot_general(
            images[k], inverse[...], (((1,), (1,)), ((), ())),
            preferred_element_type=F32, precision=lax.Precision.HIGHEST,
        ))
    start_factor(image[...], work)
    factor(0, RANK // 8)
    for cp in started:
        cp.wait_send()
    narrow = lax.dot_general(
        image[...], inverse[...], (((1,), (1,)), ((), ())),
        preferred_element_type=F32, precision=lax.Precision.HIGHEST,
    ).astype(BF16)
    out[...] = lax.dot_general(
        narrow, flat[:, pl.ds(pl.multiple_of(x * CELLS, CELLS), CELLS)],
        (((0,), (0,)), ((), ())), preferred_element_type=F32,
    )


def local(grid, slab, start):
    nzl, nx, nc, nzh, ny = (grid[k] for k in ("zl", "x", "c", "zh", "y"))
    rows = slab.shape[0]
    order = start.shape[0]
    wide = nx * CELLS
    deep = nzl * rows // ny
    dma = pltpu.SemaphoreType.DMA
    vmem = pltpu.VMEM
    core = pl.pallas_call(
        functools.partial(kernel, grid),
        out_shape=jax.ShapeDtypeStruct((RANK, CELLS), F32),
        in_specs=[pl.BlockSpec(memory_space=pltpu.HBM)] * 2,
        out_specs=pl.BlockSpec(memory_space=pltpu.VMEM),
        scratch_shapes=[
            vmem((nzl, rows, nx * nc, CELLS), F32),
            vmem((order, RANK), BF16),
            vmem((nzl, nc, rows, wide), BF16),
            vmem((order, wide), BF16),
            vmem((nc, ny, deep, order), F32),
            vmem((ny, deep, order), F32),
            vmem((ny, deep, order), F32),
            vmem((2, deep // 2, order), F32),
            vmem((2, deep, order), F32),
            vmem((nzl, CHUNK, order), F32),
            vmem((nzl, CHUNK, order), F32),
            vmem((nzh, CHUNK, order), F32),
            vmem((CHUNK, order), F32),
            vmem((nc, ny, deep, RANK), F32),
            vmem((ny, deep, RANK), F32),
            vmem((ny, deep, RANK), F32),
            vmem((ny, deep, RANK), F32),
            vmem((nzl, CHUNK, RANK), F32),
            vmem((nzl, CHUNK, RANK), F32),
            vmem((nzh, CHUNK, RANK), F32),
            vmem((ITERS, CHUNK, RANK), F32),
            vmem((order, RANK), F32),
            vmem((ITERS, order, RANK), F32),
            vmem((RANK, 2 * RANK), F32),
            vmem((RANK, RANK), F32),
            dma((nzl + 1,)), dma(()),
            dma((nzl, nc)), dma((nzl, nc)),
            dma((3, nzl, nc)), dma((3, nzl, nc)),
            dma((ny,)), dma((ny,)),
            dma((2,)), dma((2,)),
            dma((4,)), dma((4,)),
            dma((nzl,)), dma((nzl,)),
            dma((nzh,)), dma((nzh,)),
            dma(()), dma(()),
            dma((ny,)), dma((ny,)),
            dma((nzl,)), dma((nzl,)),
            dma((nzh,)), dma((nzh,)),
            dma((ITERS, nzl)), dma((ITERS, nzl)),
            dma((ITERS, nx, ny)), dma((ITERS, nx, ny)),
            dma((ITERS, nx, ny)), dma((ITERS, nx, ny)),
        ],
        compiler_params=pltpu.CompilerParams(
            collective_id=0, has_side_effects=True, vmem_limit_bytes=40 * 2**20
        ),
        name="truncate",
    )(slab.reshape(rows, nzl, nx * nc, CELLS), start)
    return core.reshape(RANK, 1, 1, CELLS)


def solution(mesh, grid=GRID):
    placed = (P("fib", "oth", None, None), P())
    return jax.shard_map(
        functools.partial(local, grid), mesh=mesh, in_specs=placed,
        out_specs=P(None, "oth", "fib", None), check_vma=False,
    )
```

time: 112 us -> 101 us (0.902)
  Pallas kernels: 109 us -> 98 us
    pallas_call x1, Pallas kernels: 109 us -> 98 us  [local(): pl.pallas_call(functools.partial(kernel, grid), out_shape=jax.ShapeDtypeS...]
where the time goes in v2:
time: 101 us
  Pallas kernels  98 us (97%)
  local copies, waits for them, and re-layouts  2.62 us (3%)
    pallas_call x1, Pallas kernels, local(): pl.pallas_call(functools.partial(kernel, grid), out_shape=jax.ShapeDtypeS...  98 us
    unnamed x5, local copies, waits for them, and re-layouts  2.62 us

profile of v2, /device:TPU:1, one launch (start us, length us, event | category | flops | bytes accessed | tf_op | source)
XLA Modules:
  0.0 100.6 jit_solution(5344777825975879072)
XLA Ops:
  0.0 0.0 copy-start
  0.0 1.0 %copy-done = f32[32,1,32,128]{3,2,1,0:T(8,128)S(1)} copy-done((f32[32,1,32,128]{3,2,1,0:T(8,128)S(1)}, f32[32,1,32,128]{3,2,1,0:T(8,128)}, u32[]{:S(2)}) %copy-start) | copy-done | bytes 524312
  1.0 0.0 copy-start.1
  1.0 0.9 copy-done.1
  2.0 98.0 %truncate.1 = f32[128,128]{1,0:T(8,128)S(1)} custom-call(f32[32,4,8,128]{3,2,1,0:T(8,128)S(1)} %bitcast.4, bf16[1024,128]{1,0:T(8,128)(2,1)S(1)} %copy-done.1), custom_call_target="tpu_custom_call" | custom-call | tf_op jit(solution)/shard_map/truncate/pallas_call | solution.py:338
  100.0 0.6 copy.5
Async XLA Ops:
  0.0 1.0 %copy-start = (f32[32,1,32,128]{3,2,1,0:T(8,128)S(1)}, f32[32,1,32,128]{3,2,1,0:T(8,128)}, u32[]{:S(2)}) copy-start(f32[32,1,32,128]{3,2,1,0:T(8,128)} %param.2) | copy-start | bytes 1572868
  1.0 0.9 copy-start.1

commit v3 on v2

v3 whole, which is shorter than its diff:
```python
import functools

import jax
import jax.numpy as jnp
from jax import lax
from jax.experimental import pallas as pl
from jax.experimental.pallas import tpu as pltpu
from jax.sharding import PartitionSpec as P

ITERS = 3
RANK = 128
CELLS = 128
CHUNK = 8
RELAYED = 4
GRID = dict(zl=4, x=4, c=2, zh=4, y=4)
MESH = pl.DeviceIdType.MESH
F32 = jnp.float32
BF16 = jnp.bfloat16


def thirds(a):
    high = a.astype(BF16)
    rest = a - high.astype(F32)
    mid = rest.astype(BF16)
    return high, mid, (rest - mid.astype(F32)).astype(BF16)


PANEL = 16
TILES = PANEL // 8


def panel_step(b, work, inverse):
    fixed = isinstance(b, int)
    base = b * PANEL if fixed else pl.multiple_of(b * PANEL, PANEL)
    left = work[pl.ds(base, PANEL), 0:RANK]
    right = work[pl.ds(base, PANEL), RANK : 2 * RANK]
    turned, at = (left, base) if fixed else (pltpu.roll(left, RANK - base, 1), 0)
    row = lax.broadcasted_iota(jnp.int32, (8, RANK), 0)
    tiles = []
    for t in range(TILES):
        rows = slice(8 * t, 8 * t + 8)
        cols = [jnp.broadcast_to(turned[rows, at + s : at + s + 1], (8, RANK)) for s in range(PANEL)]
        tiles.append(jnp.stack(cols + [left[rows], right[rows]]))
    pivots = [jnp.ones((8, RANK), F32) for _ in range(TILES)]
    for s in range(PANEL):
        ts, ss = divmod(s, 8)
        pivot = jnp.broadcast_to(tiles[ts][0, ss : ss + 1, :], (8, RANK))
        pivots[ts] = jnp.where(row == ss, pivot, pivots[ts])
        over = 1.0 / pivot
        lead = jnp.broadcast_to(tiles[ts][1:, ss : ss + 1, :], (PANEL + 1 - s, 8, RANK))
        for t in range(TILES):
            rest = tiles[t][1:]
            if t >= ts:
                factor = tiles[t][0] * over
                if t == ts:
                    factor = jnp.where(row > ss, factor, 0.0)
                rest = rest - factor[None] * lead
            tiles[t] = rest
    left = jnp.concatenate([tile[0] for tile in tiles], axis=0)
    right = jnp.concatenate([tile[1] for tile in tiles], axis=0)
    pivots = jnp.concatenate(pivots, axis=0)
    inverse[pl.ds(base, PANEL), :] = right * lax.rsqrt(pivots)
    if fixed and base + PANEL == RANK:
        return
    lane = lax.broadcasted_iota(jnp.int32, (PANEL, RANK), 1)
    factors = jnp.where(lane >= base + PANEL, left * (1.0 / pivots), 0.0)
    fh, fm, fl = thirds(factors)
    rh, rm, rl = thirds(jnp.concatenate([left, right], axis=1))
    tall = jnp.concatenate([fh, fh, fm, fh, fl, fm], axis=0)
    wide = jnp.concatenate([rh, rm, rh, rl, rh, rm], axis=0)
    change = lax.dot_general(tall, wide, (((0,), (0,)), ((), ())), preferred_element_type=F32)
    if fixed:
        work[base + PANEL :, :] = work[base + PANEL :, :] - change[base + PANEL :]
    else:
        work[...] = work[...] - change


def start_factor(image, work):
    work[:, 0:RANK] = lax.dot_general(
        image, image, (((0,), (0,)), ((), ())),
        preferred_element_type=F32, precision=lax.Precision.HIGHEST,
    )
    i0 = lax.broadcasted_iota(jnp.int32, (RANK, RANK), 0)
    i1 = lax.broadcasted_iota(jnp.int32, (RANK, RANK), 1)
    work[:, RANK : 2 * RANK] = (i0 == i1).astype(F32)


def to_unit(image):
    return image * (1.0 / jnp.max(jnp.abs(image)))


def kernel(
    grid, slab, start, out,
    stage, basis, send, flat, part, from_core, summed, from_y, chunks, from_zl, from_zh, own,
    small, s_in, s_zh, mine, image, images, work, inverse,
    load_sem, local_sem, a_send, a_recv, x_send, x_recv, c_send, c_recv, y_send, y_recv,
    zl_send, zl_recv, zh_send, zh_recv, o_send, o_recv, si_send, si_recv, sh_send, sh_recv,
    g_send, g_recv, p_send, p_recv, q_send, q_recv, near_sem, far_sem,
):
    nzl, nx, nc, nzh, ny = (grid[k] for k in ("zl", "x", "c", "zh", "y"))
    rows = stage.shape[1]
    deep = summed.shape[2]
    wide = part.shape[4]
    fib, oth = lax.axis_index("fib"), lax.axis_index("oth")
    c = lax.rem(fib, nc)
    x = lax.rem(lax.div(fib, nc), nx)
    zl = lax.div(fib, nc * nx)
    y = lax.rem(oth, ny)
    zh = lax.div(oth, ny)

    def device(dzl=0, dx=0, dc=0, dzh=0, dy=0):
        f = (lax.rem(zl + dzl, nzl) * nx + lax.rem(x + dx, nx)) * nc + lax.rem(c + dc, nc)
        o = lax.rem(zh + dzh, nzh) * ny + lax.rem(y + dy, ny)
        return (f, o)

    def along_z(d):
        z = lax.rem(zh * nzl + zl + d, nzh * nzl)
        f = (lax.rem(z, nzl) * nx + x) * nc + c
        return (f, lax.div(z, nzl) * ny + y)

    started = []

    def copy(src, dst, ssem, rsem, to):
        cp = pltpu.make_async_remote_copy(
            src_ref=src, dst_ref=dst, send_sem=ssem, recv_sem=rsem,
            device_id=to, device_id_type=MESH,
        )
        cp.start()
        started.append(cp)
        return cp

    def landed(cps):
        for cp in cps:
            cp.wait_recv()

    run = [(dz, dc) for dz in range(nzl) for dc in range(nc)]
    plane = [(dx, dy) for dx in range(nx) for dy in range(ny) if dx or dy]

    barrier = pltpu.get_barrier_semaphore()
    block_peers = [
        (dy, dz, dc) for dy in range(ny) for dz in range(nzl) for dc in range(nc) if dy or dz or dc
    ]
    chained = nzl == 4 and nzh == 4
    peers = [device(dzl=dz, dc=dc, dy=dy) for dy, dz, dc in block_peers]
    peers += [device(dx=dx) for dx in range(1, nx)]
    if chained:
        peers += [along_z(2), along_z(nzl * nzh - 2)]
    else:
        peers += [device(dzh=k) for k in range(1, nzh)]
    for peer in peers:
        pl.semaphore_signal(barrier, inc=1, device_id=peer, device_id_type=MESH)

    loads = []
    for dz in range(nzl):
        to_zl = lax.rem(zl + dz, nzl)
        load = pltpu.make_async_copy(slab.at[:, to_zl], stage.at[dz], load_sem.at[dz])
        load.start()
        loads.append(load)
    load_basis = pltpu.make_async_copy(start, basis, load_sem.at[nzl])
    load_basis.start()

    def block(dx, dz, dc):
        b = (lax.rem(zl + nzl - dz, nzl) * nx + lax.rem(x + dx, nx)) * nc + lax.rem(c + nc - dc, nc)
        return flat.at[pl.ds(pl.multiple_of(b * rows, rows), rows), :]

    here = block(0, 0, 0)
    right, left, more = {}, {}, []

    def spread(n, p, src):
        dst = block(0, *p)
        right[p] = copy(src, dst, x_send.at[0, *p], x_recv.at[0, *p], device(dx=1))
        left[p] = copy(src, dst, x_send.at[1, *p], x_recv.at[1, *p], device(dx=nx - 1))
        if n >= RELAYED:
            more.append(copy(src, dst, x_send.at[2, *p], x_recv.at[2, *p], device(dx=2)))

    def onward(n, p):
        landed([right[p], left[p]])
        if n < RELAYED:
            to, src = (1, block(nx - 1, *p)) if n % 2 == 0 else (nx - 1, block(1, *p))
            more.append(copy(src, src, x_send.at[2, *p], x_recv.at[2, *p], device(dx=to)))

    first = {}
    for dz in range(nzl):
        loads[dz].wait()
        for px in range(nx):
            v0 = stage[dz, :, px * nc, :]
            v1 = stage[dz, :, px * nc + 1, :]
            same = jnp.where(c == 0, v0, v1).astype(BF16)
            other = jnp.where(c == 0, v1, v0).astype(BF16)
            send[dz, 0, :, px * CELLS : (px + 1) * CELLS] = same
            send[dz, 1, :, px * CELLS : (px + 1) * CELLS] = other
        if dz == 0:
            pl.semaphore_wait(barrier, len(peers))
            keep = pltpu.make_async_copy(send.at[0, 0], here, local_sem)
            keep.start()
            spread(0, run[0], send.at[0, 0])
        for dc in range(nc):
            if dz or dc:
                first[dz, dc] = copy(
                    send.at[dz, dc], here, a_send.at[dz, dc], a_recv.at[dz, dc], device(dzl=dz, dc=dc)
                )
    if chained:
        for d in (2, nzl * nzh - 2):
            pl.semaphore_signal(near_sem, inc=1, device_id=along_z(d), device_id_type=MESH)
    for n, p in enumerate(run):
        if n:
            landed([first[p]])
            spread(n, p, block(0, *p))
        if n >= 4:
            onward(n - 4, run[n - 4])
    if chained:
        pl.semaphore_wait(near_sem, 2)
        for d in (nzl, nzl * nzh - nzl):
            pl.semaphore_signal(far_sem, inc=1, device_id=along_z(d), device_id_type=MESH)
    for n in range(len(run) - 4, len(run)):
        onward(n, run[n])
    landed(more)
    keep.wait()
    load_basis.wait()

    tops = jnp.concatenate([
        flat[pl.ds(pl.multiple_of(((q * nx + x) * nc + k) * rows, rows), rows), :]
        for k in range(nc) for q in range(nzl)
    ], axis=0)
    inner = lax.dot_general(
        basis[...], flat[...], (((0,), (0,)), ((), ())), preferred_element_type=F32
    )
    first_image = sum(
        lax.dot_general(tops, t, (((1,), (1,)), ((), ())), preferred_element_type=F32)
        for t in thirds(inner)[::-1]
    )
    small[...] = first_image.reshape(small.shape)
    s_in[0] = small[c, y, zl]
    small_in = []
    for n, (dy, dz, dc) in enumerate(block_peers):
        src = small.at[lax.rem(c + dc, nc), lax.rem(y + dy, ny), lax.rem(zl + dz, nzl)]
        small_in.append(
            copy(src, s_in.at[n + 1], si_send.at[n], si_recv.at[n], device(dzl=dz, dc=dc, dy=dy))
        )

    halves = range(2)
    across = []
    for h in halves:
        gram = lax.dot_general(
            tops, flat[h * wide : (h + 1) * wide, :], (((1,), (1,)), ((), ())),
            preferred_element_type=F32,
        )
        part[h] = gram.reshape(part.shape[1:])
        for d in (2, 1, 3, 0):
            q = lax.rem(y + d, ny)
            across.append((h, d, q, copy(
                part.at[h, 1 - c, q], from_core.at[h, q], c_send.at[h, d], c_recv.at[h, d], device(dc=1)
            )))

    big_y = [[], []]
    for h, d, q, cp in across:
        landed([cp])
        if d == 0:
            from_y[h, y] = part[h, c, q] + from_core[h, q]
        else:
            summed[h, q] = part[h, c, q] + from_core[h, q]
            big_y[h].append(copy(
                summed.at[h, q], from_y.at[h, y], y_send.at[h, d], y_recv.at[h, d], device(dy=d)
            ))

    landed(small_in)
    s_zh[zh] = jnp.sum(s_in[...], axis=0)
    if chained:
        pl.semaphore_wait(far_sem, 2)
    small_zh = [
        copy(s_zh.at[zh], s_zh.at[zh], sh_send.at[d], sh_recv.at[d], device(dzh=d))
        for d in range(1, nzh)
    ]

    big_zl, big_zh, big_own = [[], []], [[], []], [[], []]

    def after_y(h):
        landed(big_y[h])
        chunks[h] = sum(from_y[h, q] for q in range(ny)).reshape(chunks.shape[1:])
        from_zl[h, zl] = chunks[h, zl]
        for d in range(1, nzl):
            big_zl[h].append(copy(
                chunks.at[h, lax.rem(zl + d, nzl)], from_zl.at[h, zl],
                zl_send.at[h, d], zl_recv.at[h, d], device(dzl=d),
            ))

    def after_zl(h):
        landed(big_zl[h])
        from_zh[h, zh] = sum(from_zl[h, q] for q in range(nzl))
        for d in range(1, nzh):
            big_zh[h].append(copy(
                from_zh.at[h, zh], from_zh.at[h, zh],
                zh_send.at[h, d], zh_recv.at[h, d], device(dzh=d),
            ))

    def after_zh(h):
        landed(big_zh[h])
        own[h, zl] = sum(from_zh[h, q] for q in range(nzh))
        for d in range(1, nzl):
            big_own[h].append(copy(
                own.at[h, zl], own.at[h, zl], o_send.at[h, d], o_recv.at[h, d], device(dzl=d),
            ))

    after_y(0)
    after_y(1)
    after_zl(0)

    def place(dx, dy, core):
        rho = lax.rem(y + dy, ny) * deep
        b = (lax.div(rho, rows) * nx + lax.rem(x + dx, nx)) * nc + core
        return b * rows + lax.rem(rho, rows)

    line = nzl * CHUNK

    def block_of(k, dx, dy, core):
        return images.at[k, pl.ds(pl.multiple_of(place(dx, dy, core), line), line), :]

    def gather_start(k, value):
        mine[k] = value
        where = pl.ds(pl.multiple_of(place(0, 0, c) + zl * CHUNK, CHUNK), CHUNK)
        images[k, where, :] = value
        return [
            copy(mine.at[k], images.at[k, where, :], g_send.at[k, d], g_recv.at[k, d], device(dzl=d))
            for d in range(1, nzl)
        ]

    def gather_spread(k, cps):
        landed(cps)
        src = block_of(k, 0, 0, c)
        spread = {
            (dx, dy): copy(src, src, p_send.at[k, dx, dy], p_recv.at[k, dx, dy], device(dx=dx, dy=dy))
            for dx, dy in sorted(plane, key=lambda p: -min(p[0], nx - p[0]) - min(p[1], ny - p[1]))
        }
        return spread, [copy(src, src, q_send.at[k, 0, 0], q_recv.at[k, 0, 0], device(dc=1))]

    def gather_end(k, spread, last):
        for dx, dy in sorted(plane, key=lambda p: min(p[0], nx - p[0]) + min(p[1], ny - p[1])):
            landed([spread[dx, dy]])
            src = block_of(k, nx - dx, ny - dy, c)
            last.append(copy(src, src, q_send.at[k, dx, dy], q_recv.at[k, dx, dy], device(dc=1)))
        landed(last)

    def factor(k0, k1):
        lax.fori_loop(k0, k1, lambda b, _: (panel_step(b, work, inverse), 0)[1], 0)

    landed(small_zh)
    cps = gather_start(0, sum(s_zh[q] for q in range(nzh)))
    after_zl(1)
    both = gather_spread(0, cps)
    gather_end(0, *both)
    image[...] = to_unit(images[0])
    after_zh(0)
    after_zh(1)

    def times(mat, vec):
        return jnp.dot(mat, vec, preferred_element_type=F32, precision=lax.Precision.HIGHEST)

    for k in range(1, ITERS):
        if k == 1:
            rows_of = times(own[0, zl], image[:wide]) + times(own[1, zl], image[wide:])
            cps = gather_start(k, rows_of)
        else:
            landed(big_own[0] + big_own[1])
            rows_of = sum(times(own[h].reshape(line, wide), image[h * wide : (h + 1) * wide]) for h in halves)
            images[k, pl.ds(pl.multiple_of(place(0, 0, c), line), line), :] = rows_of
            both = gather_spread(k, [])
        start_factor(image[...], work)
        if k == 1:
            both = gather_spread(k, cps)
        factor(0, RANK // PANEL)
        gather_end(k, *both)
        image[...] = to_unit(lax.dot_general(
            images[k], inverse[...], (((1,), (1,)), ((), ())),
            preferred_element_type=F32, precision=lax.Precision.HIGHEST,
        ))
    start_factor(image[...], work)
    for b in range(RANK // PANEL):
        panel_step(b, work, inverse)
    for cp in started:
        cp.wait_send()
    narrow = lax.dot_general(
        image[...], inverse[...], (((1,), (1,)), ((), ())),
        preferred_element_type=F32, precision=lax.Precision.HIGHEST,
    ).astype(BF16)
    out[...] = lax.dot_general(
        narrow, flat[:, pl.ds(pl.multiple_of(x * CELLS, CELLS), CELLS)],
        (((0,), (0,)), ((), ())), preferred_element_type=F32,
    )


def local(grid, slab, start):
    nzl, nx, nc, nzh, ny = (grid[k] for k in ("zl", "x", "c", "zh", "y"))
    rows = slab.shape[0]
    order = start.shape[0]
    wide = order // 2
    deep = nzl * rows // ny
    dma = pltpu.SemaphoreType.DMA
    vmem = pltpu.VMEM
    core = pl.pallas_call(
        functools.partial(kernel, grid),
        out_shape=jax.ShapeDtypeStruct((RANK, CELLS), F32),
        in_specs=[pl.BlockSpec(memory_space=pltpu.HBM)] * 2,
        out_specs=pl.BlockSpec(memory_space=pltpu.VMEM),
        scratch_shapes=[
            vmem((nzl, rows, nx * nc, CELLS), F32),
            vmem((order, RANK), BF16),
            vmem((nzl, nc, rows, nx * CELLS), BF16),
            vmem((order, nx * CELLS), BF16),
            vmem((2, nc, ny, deep, wide), F32),
            vmem((2, ny, deep, wide), F32),
            vmem((2, ny, deep, wide), F32),
            vmem((2, ny, deep, wide), F32),
            vmem((2, nzl, CHUNK, wide), F32),
            vmem((2, nzl, CHUNK, wide), F32),
            vmem((2, nzh, CHUNK, wide), F32),
            vmem((2, nzl, CHUNK, wide), F32),
            vmem((nc, ny, nzl, CHUNK, RANK), F32),
            vmem((nc * ny * nzl, CHUNK, RANK), F32),
            vmem((nzh, CHUNK, RANK), F32),
            vmem((ITERS, CHUNK, RANK), F32),
            vmem((order, RANK), F32),
            vmem((ITERS, order, RANK), F32),
            vmem((RANK, 2 * RANK), F32),
            vmem((RANK, RANK), F32),
            dma((nzl + 1,)), dma(()),
            dma((nzl, nc)), dma((nzl, nc)),
            dma((3, nzl, nc)), dma((3, nzl, nc)),
            dma((2, ny)), dma((2, ny)),
            dma((2, ny)), dma((2, ny)),
            dma((2, nzl)), dma((2, nzl)),
            dma((2, nzh)), dma((2, nzh)),
            dma((2, nzl)), dma((2, nzl)),
            dma((nc * ny * nzl - 1,)), dma((nc * ny * nzl - 1,)),
            dma((nzh,)), dma((nzh,)),
            dma((ITERS, nzl)), dma((ITERS, nzl)),
            dma((ITERS, nx, ny)), dma((ITERS, nx, ny)),
            dma((ITERS, nx, ny)), dma((ITERS, nx, ny)),
            pltpu.SemaphoreType.REGULAR, pltpu.SemaphoreType.REGULAR,
        ],
        compiler_params=pltpu.CompilerParams(
            collective_id=0, has_side_effects=True, vmem_limit_bytes=60 * 2**20
        ),
        name="truncate",
    )(slab.reshape(rows, nzl, nx * nc, CELLS), start)
    return core.reshape(RANK, 1, 1, CELLS)


def solution(mesh, grid=GRID):
    placed = (P("fib", "oth", None, None), P())
    return jax.shard_map(
        functools.partial(local, grid), mesh=mesh, in_specs=placed,
        out_specs=P(None, "oth", "fib", None), check_vma=False,
    )
```

time: 101 us -> 89.2 us (0.88)
  Pallas kernels: 98 us -> 87.5 us
  local copies, waits for them, and re-layouts: 2.62 us -> 1.47 us
    pallas_call x1, Pallas kernels: 98 us -> 87.5 us  [local(): pl.pallas_call(functools.partial(kernel, grid), out_shape=jax.ShapeDtypeS...]
    unnamed x5 -> x1, local copies, waits for them, and re-layouts: 2.62 us -> 1.47 us
where the time goes in v3:
time: 89.2 us; the launch traced here: 89 us
  Pallas kernels  87.5 us (98%)
  local copies, waits for them, and re-layouts  1.47 us (2%)
    pallas_call x1, Pallas kernels, local(): pl.pallas_call(functools.partial(kernel, grid), out_shape=jax.ShapeDtypeS...  87.5 us

profile of v3, /device:TPU:1, one launch (start us, length us, event | category | flops | bytes accessed | tf_op | source)
XLA Modules:
  0.0 89.0 jit_solution(2743817987407323642)
XLA Ops:
  0.0 87.5 %truncate.1 = f32[128,128]{1,0:T(8,128)} custom-call(f32[32,4,8,128]{3,2,1,0:T(8,128)} %bitcast.4, bf16[1024,128]{1,0:T(8,128)(2,1)} %start.1), custom_call_target="tpu_custom_call" | custom-call | tf_op jit(solution)/shard_map/truncate/pallas_call | solution.py:399
  87.5 1.5 %copy.5 = f32[128,1,1,128]{3,2,1,0:T(1,128)} copy(f32[128,1,1,128]{3,2,1,0:T(1,128)} %bitcast.5) | data formatting | bytes 131072

commit v4 on v3

v4 whole, which is shorter than its diff:
```python
import functools

import jax
import jax.numpy as jnp
from jax import lax
from jax.experimental import pallas as pl
from jax.experimental.pallas import tpu as pltpu
from jax.sharding import PartitionSpec as P

ITERS = 3
RANK = 128
CELLS = 128
CHUNK = 8
GRID = dict(zl=4, x=4, c=2, zh=4, y=4)
MESH = pl.DeviceIdType.MESH
F32 = jnp.float32
BF16 = jnp.bfloat16


def thirds(a):
    high = a.astype(BF16)
    rest = a - high.astype(F32)
    mid = rest.astype(BF16)
    return high, mid, (rest - mid.astype(F32)).astype(BF16)


PANEL = 16
TILES = PANEL // 8


def panel_step(b, work, inverse):
    fixed = isinstance(b, int)
    base = b * PANEL if fixed else pl.multiple_of(b * PANEL, PANEL)
    left = work[pl.ds(base, PANEL), 0:RANK]
    right = work[pl.ds(base, PANEL), RANK : 2 * RANK]
    turned, at = (left, base) if fixed else (pltpu.roll(left, RANK - base, 1), 0)
    row = lax.broadcasted_iota(jnp.int32, (8, RANK), 0)
    tiles = []
    for t in range(TILES):
        rows = slice(8 * t, 8 * t + 8)
        cols = [jnp.broadcast_to(turned[rows, at + s : at + s + 1], (8, RANK)) for s in range(PANEL)]
        tiles.append(jnp.stack(cols + [left[rows], right[rows]]))
    pivots = [jnp.ones((8, RANK), F32) for _ in range(TILES)]
    for s in range(PANEL):
        ts, ss = divmod(s, 8)
        pivot = jnp.broadcast_to(tiles[ts][0, ss : ss + 1, :], (8, RANK))
        pivots[ts] = jnp.where(row == ss, pivot, pivots[ts])
        over = 1.0 / pivot
        lead = jnp.broadcast_to(tiles[ts][1:, ss : ss + 1, :], (PANEL + 1 - s, 8, RANK))
        for t in range(TILES):
            rest = tiles[t][1:]
            if t >= ts:
                factor = tiles[t][0] * over
                if t == ts:
                    factor = jnp.where(row > ss, factor, 0.0)
                rest = rest - factor[None] * lead
            tiles[t] = rest
    left = jnp.concatenate([tile[0] for tile in tiles], axis=0)
    right = jnp.concatenate([tile[1] for tile in tiles], axis=0)
    pivots = jnp.concatenate(pivots, axis=0)
    inverse[pl.ds(base, PANEL), :] = right * lax.rsqrt(pivots)
    if fixed and base + PANEL == RANK:
        return
    lane = lax.broadcasted_iota(jnp.int32, (PANEL, RANK), 1)
    factors = jnp.where(lane >= base + PANEL, left * (1.0 / pivots), 0.0)
    fh, fm, fl = thirds(factors)
    rh, rm, rl = thirds(jnp.concatenate([left, right], axis=1))
    tall = jnp.concatenate([fh, fh, fm, fh, fl, fm], axis=0)
    wide = jnp.concatenate([rh, rm, rh, rl, rh, rm], axis=0)
    change = lax.dot_general(tall, wide, (((0,), (0,)), ((), ())), preferred_element_type=F32)
    if fixed:
        work[base + PANEL :, :] = work[base + PANEL :, :] - change[base + PANEL :]
    else:
        work[...] = work[...] - change


def start_factor(image, work):
    work[:, 0:RANK] = lax.dot_general(
        image, image, (((0,), (0,)), ((), ())),
        preferred_element_type=F32, precision=lax.Precision.HIGHEST,
    )
    i0 = lax.broadcasted_iota(jnp.int32, (RANK, RANK), 0)
    i1 = lax.broadcasted_iota(jnp.int32, (RANK, RANK), 1)
    work[:, RANK : 2 * RANK] = (i0 == i1).astype(F32)


def to_unit(image):
    return image * (1.0 / jnp.max(jnp.abs(image)))


def kernel(
    grid, slab, start, out,
    stage, basis, send, flat, part, from_core, summed, from_y, chunks, from_zl, from_zh, own,
    small, s_in, s_line, mine, image, images, work, inverse,
    load_sem, sent, a_in, x_in, c_in, y_in, zl_in, zh_in, o_in, si_in, sl_in, g_in, p_in, q_in, near_sem, far_sem,
):
    nzl, nx, nc, nzh, ny = (grid[k] for k in ("zl", "x", "c", "zh", "y"))
    rows = stage.shape[1]
    deep = summed.shape[2]
    wide = part.shape[4]
    fib, oth = lax.axis_index("fib"), lax.axis_index("oth")
    c = lax.rem(fib, nc)
    x = lax.rem(lax.div(fib, nc), nx)
    zl = lax.div(fib, nc * nx)
    y = lax.rem(oth, ny)
    zh = lax.div(oth, ny)

    def device(dzl=0, dx=0, dc=0, dzh=0, dy=0):
        f = (lax.rem(zl + dzl, nzl) * nx + lax.rem(x + dx, nx)) * nc + lax.rem(c + dc, nc)
        o = lax.rem(zh + dzh, nzh) * ny + lax.rem(y + dy, ny)
        return (f, o)

    def along_z(d):
        z = lax.rem(zh * nzl + zl + d, nzh * nzl)
        f = (lax.rem(z, nzl) * nx + x) * nc + c
        return (f, lax.div(z, nzl) * ny + y)

    started = []

    def copy(src, dst, rsem, to):
        cp = pltpu.make_async_remote_copy(
            src_ref=src, dst_ref=dst, send_sem=sent, recv_sem=rsem,
            device_id=to, device_id_type=MESH,
        )
        cp.start()
        started.append(cp)
        return cp

    def landed(like, sem):
        pltpu.make_async_copy(like, like, sem).wait()

    run = [(dz, dc) for dz in range(nzl) for dc in range(nc)]
    plane = [(dx, dy) for dx in range(nx) for dy in range(ny) if dx or dy]

    barrier = pltpu.get_barrier_semaphore()
    block_peers = [
        (dy, dz, dc) for dy in range(ny) for dz in range(nzl) for dc in range(nc) if dy or dz or dc
    ]
    line_of = range(1, nzl * nzh)
    chained = nzl == 4 and nzh == 4
    peers = [device(dzl=dz, dc=dc, dy=dy) for dy, dz, dc in block_peers if dy == 0 or not chained]
    peers += [device(dx=dx) for dx in range(1, nx)]
    if chained:
        step_one = [along_z(2), along_z(14), device(dy=1), device(dy=ny - 1)]
        step_two = [along_z(4), along_z(12), device(dy=1), device(dy=ny - 1)]
        peers += step_one
    else:
        peers += [along_z(d) for d in line_of]
    for peer in peers:
        pl.semaphore_signal(barrier, inc=1, device_id=peer, device_id_type=MESH)

    loads = []
    for dz in range(nzl):
        to_zl = lax.rem(zl + dz, nzl)
        load = pltpu.make_async_copy(slab.at[:, to_zl], stage.at[dz], load_sem.at[dz])
        load.start()
        loads.append(load)
    load_basis = pltpu.make_async_copy(start, basis, load_sem.at[nzl])
    load_basis.start()

    halves = range(2)
    cols = nx // 2 * CELLS

    def block(h, dz, dc):
        b = (lax.rem(zl + nzl - dz, nzl) * nx + x) * nc + lax.rem(c + nc - dc, nc)
        return flat.at[h, pl.ds(pl.multiple_of(b * rows, rows), rows), :]

    def along_x(src, dst):
        for dx in (2, 1, 3):
            copy(src, dst, x_in, device(dx=dx))

    for dz in range(nzl):
        loads[dz].wait()
        for px in range(nx):
            h, at = divmod(px * CELLS, cols)
            v0 = stage[dz, :, px * nc, :]
            v1 = stage[dz, :, px * nc + 1, :]
            send[h, dz, 0, :, at : at + CELLS] = jnp.where(c == 0, v0, v1).astype(BF16)
            send[h, dz, 1, :, at : at + CELLS] = jnp.where(c == 0, v1, v0).astype(BF16)
        if dz == 0:
            keeps = [
                pltpu.make_async_copy(send.at[h, 0, 0], block(h, 0, 0), load_sem.at[nzl + 1 + h])
                for h in halves
            ]
            for keep in keeps:
                keep.start()
            pl.semaphore_wait(barrier, len(peers))
            if chained:
                for peer in step_one:
                    pl.semaphore_signal(near_sem, inc=1, device_id=peer, device_id_type=MESH)
            along_x(send.at[0, 0, 0], block(0, 0, 0))
        for dc in range(nc):
            if dz or dc:
                copy(send.at[0, dz, dc], block(0, 0, 0), a_in.at[0, dz, dc], device(dzl=dz, dc=dc))
    for dz, dc in run[1:]:
        copy(send.at[1, dz, dc], block(1, 0, 0), a_in.at[1, dz, dc], device(dzl=dz, dc=dc))
    along_x(send.at[1, 0, 0], block(1, 0, 0))
    for h in halves:
        for p in run[1:]:
            landed(block(h, *p), a_in.at[h, *p])
            along_x(block(h, *p), block(h, *p))
        if h == 0 and chained:
            pl.semaphore_wait(near_sem, len(step_one))
            for peer in step_two:
                pl.semaphore_signal(far_sem, inc=1, device_id=peer, device_id_type=MESH)
    for keep in keeps:
        keep.wait()
    load_basis.wait()
    if chained:
        pl.semaphore_wait(far_sem, len(step_two))
    landed(flat.at[:, pl.ds(0, (nx - 1) * nzl * nc * rows), :], x_in)

    tops = [
        jnp.concatenate([
            flat[h, pl.ds(pl.multiple_of(((q * nx + x) * nc + k) * rows, rows), rows), :]
            for k in range(nc) for q in range(nzl)
        ], axis=0)
        for h in halves
    ]

    def against(a, b):
        return lax.dot_general(a, b, (((1,), (1,)), ((), ())), preferred_element_type=F32)

    first_image = None
    for h in halves:
        inner = lax.dot_general(
            basis[...], flat[h], (((0,), (0,)), ((), ())), preferred_element_type=F32
        )
        for t in thirds(inner):
            term = against(tops[h], t)
            first_image = term if first_image is None else first_image + term
    small[...] = first_image.reshape(small.shape)
    s_in[0] = small[c, y, zl]
    for n, (dy, dz, dc) in enumerate(block_peers):
        src = small.at[lax.rem(c + dc, nc), lax.rem(y + dy, ny), lax.rem(zl + dz, nzl)]
        copy(src, s_in.at[n + 1], si_in, device(dzl=dz, dc=dc, dy=dy))

    for h in halves:
        span = slice(h * wide, (h + 1) * wide)
        part[h] = sum(against(tops[g], flat[g, span, :]) for g in halves).reshape(part.shape[1:])
        for d in (2, 1, 3, 0):
            q = lax.rem(y + d, ny)
            copy(part.at[h, 1 - c, q], from_core.at[h, q], c_in.at[h], device(dc=1))

    for h in halves:
        landed(from_core.at[h], c_in.at[h])
        for d in (2, 1, 3, 0):
            q = lax.rem(y + d, ny)
            if d == 0:
                from_y[h, y] = part[h, c, q] + from_core[h, q]
            else:
                summed[h, q] = part[h, c, q] + from_core[h, q]
                copy(summed.at[h, q], from_y.at[h, y], y_in.at[h], device(dy=d))

    landed(s_in.at[1:], si_in)
    place_z = zh * nzl + zl
    s_line[place_z] = jnp.sum(s_in[...], axis=0)
    for d in sorted(line_of, key=lambda d: -min(d, nzl * nzh - d)):
        copy(s_line.at[place_z], s_line.at[place_z], sl_in, along_z(d))

    def after_y(h):
        landed(from_y.at[h, 1:], y_in.at[h])
        chunks[h] = sum(from_y[h, q] for q in range(ny)).reshape(chunks.shape[1:])
        from_zl[h, zl] = chunks[h, zl]
        for d in range(1, nzl):
            copy(chunks.at[h, lax.rem(zl + d, nzl)], from_zl.at[h, zl], zl_in.at[h], device(dzl=d))

    def after_zl(h):
        landed(from_zl.at[h, 1:], zl_in.at[h])
        from_zh[h, zh] = sum(from_zl[h, q] for q in range(nzl))
        for d in range(1, nzh):
            copy(from_zh.at[h, zh], from_zh.at[h, zh], zh_in.at[h], device(dzh=d))

    def after_zh(h):
        landed(from_zh.at[h, 1:], zh_in.at[h])
        own[h, zl] = sum(from_zh[h, q] for q in range(nzh))
        for d in range(1, nzl):
            copy(own.at[h, zl], own.at[h, zl], o_in, device(dzl=d))

    after_y(0)
    after_y(1)
    after_zl(0)

    def place(dx, dy, core):
        rho = lax.rem(y + dy, ny) * deep
        b = (lax.div(rho, rows) * nx + lax.rem(x + dx, nx)) * nc + core
        return b * rows + lax.rem(rho, rows)

    line = nzl * CHUNK

    def block_of(k, dx, dy, core):
        return images.at[k, pl.ds(pl.multiple_of(place(dx, dy, core), line), line), :]

    def hops(p):
        return min(p[0], nx - p[0]) + min(p[1], ny - p[1])

    def gather_start(k, value):
        mine[k] = value
        where = pl.ds(pl.multiple_of(place(0, 0, c) + zl * CHUNK, CHUNK), CHUNK)
        images[k, where, :] = value
        for d in range(1, nzl):
            copy(mine.at[k], images.at[k, where, :], g_in, device(dzl=d))

    def gather_spread(k):
        src = block_of(k, 0, 0, c)
        for p in sorted(plane, key=lambda p: -hops(p)):
            copy(src, src, p_in.at[k, int(hops(p) > 2)], device(dx=p[0], dy=p[1]))
        copy(src, src, q_in.at[k], device(dc=1))

    def gather_pass(k, far):
        group = [p for p in plane if (hops(p) > 2) == far]
        landed(images.at[k, pl.ds(0, len(group) * line), :], p_in.at[k, int(far)])
        for dx, dy in group:
            src = block_of(k, nx - dx, ny - dy, c)
            copy(src, src, q_in.at[k], device(dc=1))

    def gather_end(k):
        landed(images.at[k, pl.ds(0, nx * ny * line), :], q_in.at[k])

    def factor(k0, k1):
        lax.fori_loop(k0, k1, lambda b, _: (panel_step(b, work, inverse), 0)[1], 0)

    landed(s_line.at[1:], sl_in)
    mine_rows = pl.ds(pl.multiple_of(place(0, 0, c), line), line)
    images[0, mine_rows, :] = sum(
        s_line[q * nzl : (q + 1) * nzl] for q in range(nzh)
    ).reshape(line, RANK)
    gather_spread(0)
    after_zl(1)
    gather_pass(0, False)
    gather_pass(0, True)
    gather_end(0)
    image[...] = to_unit(images[0])
    after_zh(0)
    after_zh(1)

    def times(mat, vec):
        return jnp.dot(mat, vec, preferred_element_type=F32, precision=lax.Precision.HIGHEST)

    for k in range(1, ITERS):
        if k == 1:
            gather_start(k, times(own[0, zl], image[:wide]) + times(own[1, zl], image[wide:]))
            start_factor(image[...], work)
            factor(0, 2)
            landed(images.at[k, pl.ds(0, (nzl - 1) * CHUNK), :], g_in)
            gather_spread(k)
            factor(2, 7)
        else:
            landed(own.at[:, 1:], o_in)
            images[k, mine_rows, :] = sum(
                times(own[h].reshape(line, wide), image[h * wide : (h + 1) * wide]) for h in halves
            )
            gather_spread(k)
            start_factor(image[...], work)
            factor(0, 5)
        gather_pass(k, False)
        factor(7 if k == 1 else 5, RANK // PANEL)
        gather_pass(k, True)
        gather_end(k)
        image[...] = to_unit(lax.dot_general(
            images[k], inverse[...], (((1,), (1,)), ((), ())),
            preferred_element_type=F32, precision=lax.Precision.HIGHEST,
        ))
    start_factor(image[...], work)
    for b in range(RANK // PANEL):
        panel_step(b, work, inverse)
    for cp in started:
        cp.wait_send()
    narrow = lax.dot_general(
        image[...], inverse[...], (((1,), (1,)), ((), ())),
        preferred_element_type=F32, precision=lax.Precision.HIGHEST,
    ).astype(BF16)
    out[...] = lax.dot_general(
        narrow,
        flat[lax.div(x, nx // 2), :, pl.ds(pl.multiple_of(lax.rem(x, nx // 2) * CELLS, CELLS), CELLS)],
        (((0,), (0,)), ((), ())), preferred_element_type=F32,
    )


def local(grid, slab, start):
    nzl, nx, nc, nzh, ny = (grid[k] for k in ("zl", "x", "c", "zh", "y"))
    rows = slab.shape[0]
    order = start.shape[0]
    wide = order // 2
    deep = nzl * rows // ny
    dma = pltpu.SemaphoreType.DMA
    vmem = pltpu.VMEM
    core = pl.pallas_call(
        functools.partial(kernel, grid),
        out_shape=jax.ShapeDtypeStruct((RANK, CELLS), F32),
        in_specs=[pl.BlockSpec(memory_space=pltpu.HBM)] * 2,
        out_specs=pl.BlockSpec(memory_space=pltpu.VMEM),
        scratch_shapes=[
            vmem((nzl, rows, nx * nc, CELLS), F32),
            vmem((order, RANK), BF16),
            vmem((2, nzl, nc, rows, nx // 2 * CELLS), BF16),
            vmem((2, order, nx // 2 * CELLS), BF16),
            vmem((2, nc, ny, deep, wide), F32),
            vmem((2, ny, deep, wide), F32),
            vmem((2, ny, deep, wide), F32),
            vmem((2, ny, deep, wide), F32),
            vmem((2, nzl, CHUNK, wide), F32),
            vmem((2, nzl, CHUNK, wide), F32),
            vmem((2, nzh, CHUNK, wide), F32),
            vmem((2, nzl, CHUNK, wide), F32),
            vmem((nc, ny, nzl, CHUNK, RANK), F32),
            vmem((nc * ny * nzl, CHUNK, RANK), F32),
            vmem((nzh * nzl, CHUNK, RANK), F32),
            vmem((ITERS, CHUNK, RANK), F32),
            vmem((order, RANK), F32),
            vmem((ITERS, order, RANK), F32),
            vmem((RANK, 2 * RANK), F32),
            vmem((RANK, RANK), F32),
            dma((nzl + 3,)), dma(()),
            dma((2, nzl, nc)), dma(()), dma((2,)), dma((2,)), dma((2,)), dma((2,)),
            dma(()), dma(()), dma(()), dma(()), dma((ITERS, 2)), dma((ITERS,)),
            pltpu.SemaphoreType.REGULAR, pltpu.SemaphoreType.REGULAR,
        ],
        compiler_params=pltpu.CompilerParams(
            collective_id=0, has_side_effects=True, vmem_limit_bytes=55104 * 2**10
        ),
        name="truncate",
    )(slab.reshape(rows, nzl, nx * nc, CELLS), start)
    return core.reshape(RANK, 1, 1, CELLS)


def solution(mesh, grid=GRID):
    placed = (P("fib", "oth", None, None), P())
    return jax.shard_map(
        functools.partial(local, grid), mesh=mesh, in_specs=placed,
        out_specs=P(None, "oth", "fib", None), check_vma=False,
    )
```

time: 89.2 us -> 82.5 us (0.925)
  Pallas kernels: 87.5 us -> 81.7 us
    pallas_call x1, Pallas kernels: 87.5 us -> 81.7 us  [local(): pl.pallas_call(functools.partial(kernel, grid), out_shape=jax.ShapeDtypeS...]
where the time goes in v4:
time: 82.5 us; the launch traced here: 82.4 us
  Pallas kernels  81.7 us (99%)
    pallas_call x1, Pallas kernels, local(): pl.pallas_call(functools.partial(kernel, grid), out_shape=jax.ShapeDtypeS...  81.7 us

profile of v4, /device:TPU:1, one launch (start us, length us, event | category | flops | bytes accessed | tf_op | source)
XLA Modules:
  0.0 82.4 jit_solution(12753415061200450122)
XLA Ops:
  0.0 81.7 %truncate.1 = f32[128,128]{1,0:T(8,128)S(1)} custom-call(f32[32,4,8,128]{3,2,1,0:T(8,128)} %bitcast.5, bf16[1024,128]{1,0:T(8,128)(2,1)} %start.1), custom_call_target="tpu_custom_call" | custom-call | tf_op jit(solution)/shard_map/truncate/pallas_call | solution.py:388
  81.7 0.6 copy.5

commit v5 on v4

v5 whole, which is shorter than its diff:
```python
import functools

import jax
import jax.numpy as jnp
from jax import lax
from jax.experimental import pallas as pl
from jax.experimental.pallas import tpu as pltpu
from jax.sharding import PartitionSpec as P

ITERS = 3
RANK = 128
CELLS = 128
CHUNK = 8
GRID = dict(zl=4, x=4, c=2, zh=4, y=4)
MESH = pl.DeviceIdType.MESH
F32 = jnp.float32
BF16 = jnp.bfloat16


def thirds(a):
    high = a.astype(BF16)
    rest = a - high.astype(F32)
    mid = rest.astype(BF16)
    return high, mid, (rest - mid.astype(F32)).astype(BF16)


PANEL = 16
TILES = PANEL // 8


def panel_step(b, work, inverse):
    fixed = isinstance(b, int)
    base = b * PANEL if fixed else pl.multiple_of(b * PANEL, PANEL)
    left = work[pl.ds(base, PANEL), 0:RANK]
    right = work[pl.ds(base, PANEL), RANK : 2 * RANK]
    turned, at = (left, base) if fixed else (pltpu.roll(left, RANK - base, 1), 0)
    row = lax.broadcasted_iota(jnp.int32, (8, RANK), 0)
    tiles = []
    for t in range(TILES):
        rows = slice(8 * t, 8 * t + 8)
        cols = [jnp.broadcast_to(turned[rows, at + s : at + s + 1], (8, RANK)) for s in range(PANEL)]
        tiles.append(jnp.stack(cols + [left[rows], right[rows]]))
    pivots = [jnp.ones((8, RANK), F32) for _ in range(TILES)]
    for s in range(PANEL):
        ts, ss = divmod(s, 8)
        pivot = jnp.broadcast_to(tiles[ts][0, ss : ss + 1, :], (8, RANK))
        pivots[ts] = jnp.where(row == ss, pivot, pivots[ts])
        over = 1.0 / pivot
        lead = jnp.broadcast_to(tiles[ts][1:, ss : ss + 1, :], (PANEL + 1 - s, 8, RANK))
        for t in range(TILES):
            rest = tiles[t][1:]
            if t >= ts:
                factor = tiles[t][0] * over
                if t == ts:
                    factor = jnp.where(row > ss, factor, 0.0)
                rest = rest - factor[None] * lead
            tiles[t] = rest
    left = jnp.concatenate([tile[0] for tile in tiles], axis=0)
    right = jnp.concatenate([tile[1] for tile in tiles], axis=0)
    pivots = jnp.concatenate(pivots, axis=0)
    inverse[pl.ds(base, PANEL), :] = right * lax.rsqrt(pivots)
    if fixed and base + PANEL == RANK:
        return
    lane = lax.broadcasted_iota(jnp.int32, (PANEL, RANK), 1)
    factors = jnp.where(lane >= base + PANEL, left * (1.0 / pivots), 0.0)
    fh, fm, fl = thirds(factors)
    rh, rm, rl = thirds(jnp.concatenate([left, right], axis=1))
    tall = jnp.concatenate([fh, fh, fm, fh, fl, fm], axis=0)
    wide = jnp.concatenate([rh, rm, rh, rl, rh, rm], axis=0)
    change = lax.dot_general(tall, wide, (((0,), (0,)), ((), ())), preferred_element_type=F32)
    if fixed:
        work[base + PANEL :, :] = work[base + PANEL :, :] - change[base + PANEL :]
    else:
        work[...] = work[...] - change


def start_factor(image, work):
    work[:, 0:RANK] = lax.dot_general(
        image, image, (((0,), (0,)), ((), ())),
        preferred_element_type=F32, precision=lax.Precision.HIGHEST,
    )
    i0 = lax.broadcasted_iota(jnp.int32, (RANK, RANK), 0)
    i1 = lax.broadcasted_iota(jnp.int32, (RANK, RANK), 1)
    work[:, RANK : 2 * RANK] = (i0 == i1).astype(F32)


def to_unit(image):
    return image * (1.0 / jnp.max(jnp.abs(image)))


def kernel(
    grid, slab, start, out,
    stage, basis, send, flat, part, from_core, summed, from_y, chunks, from_zl, from_zh, own,
    small, s_in, s_line, image, images, work, inverse,
    load_sem, sent, a_in, x_in, c_in, y_in, zl_in, zh_in, o_in, si_in, sl_in, p_in, q_in, near_sem, far_sem,
):
    nzl, nx, nc, nzh, ny = (grid[k] for k in ("zl", "x", "c", "zh", "y"))
    rows = stage.shape[1]
    wide = part.shape[4]
    fib, oth = lax.axis_index("fib"), lax.axis_index("oth")
    c = lax.rem(fib, nc)
    x = lax.rem(lax.div(fib, nc), nx)
    zl = lax.div(fib, nc * nx)
    y = lax.rem(oth, ny)
    zh = lax.div(oth, ny)

    def device(dzl=0, dx=0, dc=0, dzh=0, dy=0):
        f = (lax.rem(zl + dzl, nzl) * nx + lax.rem(x + dx, nx)) * nc + lax.rem(c + dc, nc)
        o = lax.rem(zh + dzh, nzh) * ny + lax.rem(y + dy, ny)
        return (f, o)

    def along_z(d):
        z = lax.rem(zh * nzl + zl + d, nzh * nzl)
        f = (lax.rem(z, nzl) * nx + x) * nc + c
        return (f, lax.div(z, nzl) * ny + y)

    started = []

    def copy(src, dst, rsem, to):
        cp = pltpu.make_async_remote_copy(
            src_ref=src, dst_ref=dst, send_sem=sent, recv_sem=rsem,
            device_id=to, device_id_type=MESH,
        )
        cp.start()
        started.append(cp)
        return cp

    def landed(like, sem):
        pltpu.make_async_copy(like, like, sem).wait()

    run = [(dz, dc) for dz in range(nzl) for dc in range(nc)]
    plane = [(dx, dy) for dx in range(nx) for dy in range(ny) if dx or dy]

    barrier = pltpu.get_barrier_semaphore()
    block_peers = [
        (dy, dz, dc) for dy in range(ny) for dz in range(nzl) for dc in range(nc) if dy or dz or dc
    ]
    line_of = range(1, nzl * nzh)
    chained = nzl == 4 and nzh == 4
    peers = [device(dzl=dz, dc=dc, dy=dy) for dy, dz, dc in block_peers if dy == 0 or not chained]
    peers += [device(dx=dx) for dx in range(1, nx)]
    if chained:
        step_one = [along_z(2), along_z(14), device(dy=1), device(dy=ny - 1)]
        step_two = [along_z(4), along_z(12), device(dy=1), device(dy=ny - 1)]
        peers += step_one
    else:
        peers += [along_z(d) for d in line_of]
    for peer in peers:
        pl.semaphore_signal(barrier, inc=1, device_id=peer, device_id_type=MESH)

    loads = []
    for dz in range(nzl):
        to_zl = lax.rem(zl + dz, nzl)
        load = pltpu.make_async_copy(slab.at[:, to_zl], stage.at[dz], load_sem.at[dz])
        load.start()
        loads.append(load)
    for k in range(nx):
        load = pltpu.make_async_copy(start.at[:, k], basis.at[k], load_sem.at[nzl + k])
        load.start()
        loads.append(load)

    def block(dx, dz, dc):
        b = (lax.rem(x + dx, nx) * nzl + lax.rem(zl + nzl - dz, nzl)) * nc + lax.rem(c + nc - dc, nc)
        return flat.at[pl.ds(pl.multiple_of(b * rows, rows), rows), :]

    def quarter(dx):
        return pl.ds(pl.multiple_of(lax.rem(x + dx, nx) * wide, wide), wide)

    here = block(0, 0, 0)
    keep = pltpu.make_async_copy(send.at[0, 0], here, load_sem.at[nzl + nx])
    for dz in range(nzl):
        loads[dz].wait()
        for px in range(nx):
            v0 = stage[dz, :, px * nc, :]
            v1 = stage[dz, :, px * nc + 1, :]
            send[dz, 0, :, px * CELLS : (px + 1) * CELLS] = jnp.where(c == 0, v0, v1).astype(BF16)
            send[dz, 1, :, px * CELLS : (px + 1) * CELLS] = jnp.where(c == 0, v1, v0).astype(BF16)
        if dz == 0:
            keep.start()
            pl.semaphore_wait(barrier, len(peers))
            if chained:
                for peer in step_one:
                    pl.semaphore_signal(near_sem, inc=1, device_id=peer, device_id_type=MESH)
        for dc in range(nc):
            if dz or dc:
                copy(send.at[dz, dc], here, a_in.at[dz, dc], device(dzl=dz, dc=dc))
        if dz == 0:
            copy(send.at[0, 0], here, x_in.at[0], device(dx=1))
            copy(send.at[0, 0], here, x_in.at[1], device(dx=nx - 1))
    for p in run[1:]:
        piece = block(0, *p)
        landed(piece, a_in.at[p])
        copy(piece, piece, x_in.at[0], device(dx=1))
        copy(piece, piece, x_in.at[1], device(dx=nx - 1))
    if chained:
        pl.semaphore_wait(near_sem, len(step_one))
        for peer in step_two:
            pl.semaphore_signal(far_sem, inc=1, device_id=peer, device_id_type=MESH)
    keep.wait()
    for load in loads[nzl:]:
        load.wait()

    def against(a, b):
        return lax.dot_general(a, b, (((1,), (1,)), ((), ())), preferred_element_type=F32)

    tops = jnp.concatenate([
        flat[pl.ds(pl.multiple_of(((x * nzl + q) * nc + k) * rows, rows), rows), :]
        for k in range(nc) for q in range(nzl)
    ], axis=0)

    def gram(d):
        part[d] = against(tops, flat[quarter(d), :]).reshape(part.shape[1:])
        copy(part.at[d, 1 - c], from_core.at[d], c_in.at[d], device(dc=1))

    def after_core(d):
        landed(from_core.at[d], c_in.at[d])
        for dy in (2, 1, 3, 0):
            q = lax.rem(y + dy, ny)
            if dy == 0:
                from_y[d, y] = part[d, c, q] + from_core[d, q]
            else:
                summed[d, q] = part[d, c, q] + from_core[d, q]
                copy(summed.at[d, q], from_y.at[d, y], y_in.at[d], device(dy=dy))

    def after_y(d):
        landed(from_y.at[d, 1:], y_in.at[d])
        chunks[d] = sum(from_y[d, q] for q in range(ny)).reshape(chunks.shape[1:])
        from_zl[d, zl] = chunks[d, zl]
        for dz in range(1, nzl):
            copy(chunks.at[d, lax.rem(zl + dz, nzl)], from_zl.at[d, zl], zl_in.at[d], device(dzl=dz))

    def after_zl(d):
        landed(from_zl.at[d, 1:], zl_in.at[d])
        from_zh[d, zh] = sum(from_zl[d, q] for q in range(nzl))
        for dz in range(1, nzh):
            copy(from_zh.at[d, zh], from_zh.at[d, zh], zh_in.at[d], device(dzh=dz))

    def after_zh(d):
        landed(from_zh.at[d, 1:], zh_in.at[d])
        own[d, zl] = sum(from_zh[d, q] for q in range(nzh))
        for dz in range(1, nzl):
            copy(own.at[d, zl], own.at[d, zl], o_in, device(dzl=dz))

    def weigh(d):
        return lax.dot_general(
            basis[lax.rem(x + d, nx)].reshape(wide, RANK), flat[quarter(d), :],
            (((0,), (0,)), ((), ())), preferred_element_type=F32,
        )

    def relay(d, core, dx):
        for q in range(nzl):
            b = (lax.rem(x + d, nx) * nzl + q) * nc + core
            piece = flat.at[pl.ds(pl.multiple_of(b * rows, rows), rows), :]
            copy(piece, piece, x_in.at[2], device(dx=dx))

    gram(0)
    landed(flat.at[quarter(nx - 1), :], x_in.at[0])
    relay(nx - 1, 0, 1)
    landed(flat.at[quarter(1), :], x_in.at[1])
    relay(1, 1, nx - 1)
    gram(3)
    gram(1)
    inner = weigh(0) + weigh(3) + weigh(1)
    after_core(0)
    after_core(3)
    after_core(1)
    after_y(0)
    if chained:
        pl.semaphore_wait(far_sem, len(step_two))
    landed(flat.at[quarter(2), :], x_in.at[2])

    inner = inner + weigh(2)
    first_image = sum(against(tops, t) for t in thirds(inner)[::-1])
    small[...] = first_image.reshape(small.shape)
    s_in[0] = small[c, y, zl]
    for n, (dy, dz, dc) in enumerate(block_peers):
        src = small.at[lax.rem(c + dc, nc), lax.rem(y + dy, ny), lax.rem(zl + dz, nzl)]
        copy(src, s_in.at[n + 1], si_in, device(dzl=dz, dc=dc, dy=dy))
    gram(2)
    after_y(3)
    after_y(1)
    after_core(2)
    after_zl(0)
    after_y(2)

    landed(s_in.at[1:], si_in)
    place_z = zh * nzl + zl
    s_line[place_z] = jnp.sum(s_in[...], axis=0)
    for d in sorted(line_of, key=lambda d: -min(d, nzl * nzh - d)):
        copy(s_line.at[place_z], s_line.at[place_z], sl_in, along_z(d))
    after_zl(3)
    after_zl(1)
    after_zl(2)
    after_zh(0)

    line = nzl * CHUNK

    def place(dx, dy, core):
        b = (lax.rem(x + dx, nx) * nzl + lax.rem(y + dy, ny)) * nc + core
        return pl.ds(pl.multiple_of(b * line, line), line)

    mine = place(0, 0, c)

    def hops(p):
        return min(p[0], nx - p[0]) + min(p[1], ny - p[1])

    def gather_spread(k):
        src = images.at[k, mine, :]
        for p in sorted(plane, key=lambda p: -hops(p)):
            copy(src, src, p_in.at[k, int(hops(p) > 2)], device(dx=p[0], dy=p[1]))
        copy(src, src, q_in.at[k], device(dc=1))

    def gather_pass(k, far):
        group = [p for p in plane if (hops(p) > 2) == far]
        landed(images.at[k, pl.ds(0, len(group) * line), :], p_in.at[k, int(far)])
        for dx, dy in group:
            src = images.at[k, place(nx - dx, ny - dy, c), :]
            copy(src, src, q_in.at[k], device(dc=1))

    def gather_end(k):
        landed(images.at[k, pl.ds(0, nx * ny * line), :], q_in.at[k])

    def factor(k0, k1):
        lax.fori_loop(k0, k1, lambda b, _: (panel_step(b, work, inverse), 0)[1], 0)

    landed(s_line.at[1:], sl_in)
    images[0, mine, :] = sum(
        s_line[q * nzl : (q + 1) * nzl] for q in range(nzh)
    ).reshape(line, RANK)
    gather_spread(0)
    after_zh(3)
    after_zh(1)
    gather_pass(0, False)
    after_zh(2)
    gather_pass(0, True)
    gather_end(0)
    image[...] = to_unit(images[0])
    landed(own.at[:, 1:], o_in)

    for k in range(1, ITERS):
        images[k, mine, :] = sum(
            jnp.dot(own[d].reshape(line, wide), image[quarter(d), :],
                    preferred_element_type=F32, precision=lax.Precision.HIGHEST)
            for d in range(nx)
        )
        gather_spread(k)
        start_factor(image[...], work)
        factor(0, 5)
        gather_pass(k, False)
        factor(5, RANK // PANEL)
        gather_pass(k, True)
        if k == ITERS - 1:
            waited = len(started) - nx * ny
            for cp in started[:waited]:
                cp.wait_send()
        gather_end(k)
        image[...] = to_unit(lax.dot_general(
            images[k], inverse[...], (((1,), (1,)), ((), ())),
            preferred_element_type=F32, precision=lax.Precision.HIGHEST,
        ))
    start_factor(image[...], work)
    for b in range(RANK // PANEL):
        panel_step(b, work, inverse)
    for cp in started[waited:]:
        cp.wait_send()
    narrow = lax.dot_general(
        image[...], inverse[...], (((1,), (1,)), ((), ())),
        preferred_element_type=F32, precision=lax.Precision.HIGHEST,
    ).astype(BF16)
    out[...] = lax.dot_general(
        narrow, flat[:, pl.ds(pl.multiple_of(x * CELLS, CELLS), CELLS)],
        (((0,), (0,)), ((), ())), preferred_element_type=F32,
    )


def local(grid, slab, start):
    nzl, nx, nc, nzh, ny = (grid[k] for k in ("zl", "x", "c", "zh", "y"))
    rows = slab.shape[0]
    order = start.shape[0]
    wide = order // nx
    deep = nzl * rows // ny
    dma = pltpu.SemaphoreType.DMA
    vmem = pltpu.VMEM
    core = pl.pallas_call(
        functools.partial(kernel, grid),
        out_shape=jax.ShapeDtypeStruct((RANK, CELLS), F32),
        in_specs=[pl.BlockSpec(memory_space=pltpu.HBM)] * 2,
        out_specs=pl.BlockSpec(memory_space=pltpu.VMEM),
        scratch_shapes=[
            vmem((nzl, rows, nx * nc, CELLS), F32),
            vmem((nx, nzl, nc * rows, RANK), BF16),
            vmem((nzl, nc, rows, nx * CELLS), BF16),
            vmem((order, nx * CELLS), BF16),
            vmem((nx, nc, ny, deep, wide), F32),
            vmem((nx, ny, deep, wide), F32),
            vmem((nx, ny, deep, wide), F32),
            vmem((nx, ny, deep, wide), F32),
            vmem((nx, nzl, CHUNK, wide), F32),
            vmem((nx, nzl, CHUNK, wide), F32),
            vmem((nx, nzh, CHUNK, wide), F32),
            vmem((nx, nzl, CHUNK, wide), F32),
            vmem((nc, ny, nzl, CHUNK, RANK), F32),
            vmem((nc * ny * nzl, CHUNK, RANK), F32),
            vmem((nzh * nzl, CHUNK, RANK), F32),
            vmem((order, RANK), F32),
            vmem((ITERS, order, RANK), F32),
            vmem((RANK, 2 * RANK), F32),
            vmem((RANK, RANK), F32),
            dma((nzl + nx + 1,)), dma(()),
            dma((nzl, nc)), dma((3,)), dma((nx,)), dma((nx,)), dma((nx,)), dma((nx,)),
            dma(()), dma(()), dma(()), dma((ITERS, 2)), dma((ITERS,)),
            pltpu.SemaphoreType.REGULAR, pltpu.SemaphoreType.REGULAR,
        ],
        compiler_params=pltpu.CompilerParams(
            collective_id=0, has_side_effects=True, vmem_limit_bytes=55104 * 2**10
        ),
        name="truncate",
    )(slab.reshape(rows, nzl, nx * nc, CELLS), start.reshape(nzl, nx, nc * rows, RANK))
    return core.reshape(RANK, 1, 1, CELLS)


def solution(mesh, grid=GRID):
    placed = (P("fib", "oth", None, None), P())
    return jax.shard_map(
        functools.partial(local, grid), mesh=mesh, in_specs=placed,
        out_specs=P(None, "oth", "fib", None), check_vma=False,
    )
```

time: 82.5 us -> 82 us (level)
  no operation moved by 1% of the time
where the time goes in v5:
time: 82 us; the launch traced here: 81.9 us
  Pallas kernels  81.3 us (99%)
    pallas_call x1, Pallas kernels, local(): pl.pallas_call(functools.partial(kernel, grid), out_shape=jax.ShapeDtypeS...  81.3 us

profile of v5, /device:TPU:1, one launch (start us, length us, event | category | flops | bytes accessed | tf_op | source)
XLA Modules:
  0.0 81.9 jit_solution(7681504799397321890)
XLA Ops:
  0.0 81.3 %truncate.1 = f32[128,128]{1,0:T(8,128)S(1)} custom-call(f32[32,4,8,128]{3,2,1,0:T(8,128)} %bitcast.6, bf16[4,4,64,128]{3,2,1,0:T(8,128)(2,1)} %bitcast.7), custom_call_target="tpu_custom_call" | custom-call | tf_op jit(solution)/shard_map/truncate/pallas_call | solution.py:384
  81.3 0.6 copy.5

commit v6 on v5

--- a/solution.py
+++ b/solution.py
@@ -131,6 +131,12 @@
     run = [(dz, dc) for dz in range(nzl) for dc in range(nc)]
     plane = [(dx, dy) for dx in range(nx) for dy in range(ny) if dx or dy]
 
+    loads = []
+    for dz in range(nzl):
+        to_zl = lax.rem(zl + dz, nzl)
+        load = pltpu.make_async_copy(slab.at[:, to_zl], stage.at[dz], load_sem.at[dz])
+        load.start()
+        loads.append(load)
     barrier = pltpu.get_barrier_semaphore()
     block_peers = [
         (dy, dz, dc) for dy in range(ny) for dz in range(nzl) for dc in range(nc) if dy or dz or dc
@@ -148,12 +154,6 @@
     for peer in peers:
         pl.semaphore_signal(barrier, inc=1, device_id=peer, device_id_type=MESH)
 
-    loads = []
-    for dz in range(nzl):
-        to_zl = lax.rem(zl + dz, nzl)
-        load = pltpu.make_async_copy(slab.at[:, to_zl], stage.at[dz], load_sem.at[dz])
-        load.start()
-        loads.append(load)
     for k in range(nx):
         load = pltpu.make_async_copy(start.at[:, k], basis.at[k], load_sem.at[nzl + k])
         load.start()
@@ -273,7 +273,8 @@
     first_image = sum(against(tops, t) for t in thirds(inner)[::-1])
     small[...] = first_image.reshape(small.shape)
     s_in[0] = small[c, y, zl]
-    for n, (dy, dz, dc) in enumerate(block_peers):
+    reach = lambda p: min(p[0], ny - p[0]) + min(p[1], nzl - p[1])
+    for n, (dy, dz, dc) in sorted(enumerate(block_peers), key=lambda p: -reach(p[1])):
         src = small.at[lax.rem(c + dc, nc), lax.rem(y + dy, ny), lax.rem(zl + dz, nzl)]
         copy(src, s_in.at[n + 1], si_in, device(dzl=dz, dc=dc, dy=dy))
     gram(2)
@@ -291,7 +292,6 @@
     after_zl(3)
     after_zl(1)
     after_zl(2)
-    after_zh(0)
 
     line = nzl * CHUNK
 
@@ -328,6 +328,7 @@
         s_line[q * nzl : (q + 1) * nzl] for q in range(nzh)
     ).reshape(line, RANK)
     gather_spread(0)
+    after_zh(0)
     after_zh(3)
     after_zh(1)
     gather_pass(0, False)
@@ -335,24 +336,19 @@
     gather_pass(0, True)
     gather_end(0)
     image[...] = to_unit(images[0])
+
+    def times(strip, d):
+        return jnp.dot(strip, image[quarter(d), :], preferred_element_type=F32, precision=lax.Precision.HIGHEST)
+
     landed(own.at[:, 1:], o_in)
-
     for k in range(1, ITERS):
-        images[k, mine, :] = sum(
-            jnp.dot(own[d].reshape(line, wide), image[quarter(d), :],
-                    preferred_element_type=F32, precision=lax.Precision.HIGHEST)
-            for d in range(nx)
-        )
+        images[k, mine, :] = sum(times(own[d].reshape(line, wide), d) for d in range(nx))
         gather_spread(k)
         start_factor(image[...], work)
         factor(0, 5)
         gather_pass(k, False)
         factor(5, RANK // PANEL)
         gather_pass(k, True)
-        if k == ITERS - 1:
-            waited = len(started) - nx * ny
-            for cp in started[:waited]:
-                cp.wait_send()
         gather_end(k)
         image[...] = to_unit(lax.dot_general(
             images[k], inverse[...], (((1,), (1,)), ((), ())),
@@ -361,7 +357,7 @@
     start_factor(image[...], work)
     for b in range(RANK // PANEL):
         panel_step(b, work, inverse)
-    for cp in started[waited:]:
+    for cp in started:
         cp.wait_send()
     narrow = lax.dot_general(
         image[...], inverse[...], (((1,), (1,)), ((), ())),

time: 82 us -> 81.6 us (level)
  no operation moved by 1% of the time
where the time goes in v6:
time: 81.6 us; the launch traced here: 81.5 us
  Pallas kernels  80.9 us (99%)
    pallas_call x1, Pallas kernels, local(): pl.pallas_call(functools.partial(kernel, grid), out_shape=jax.ShapeDtypeS...  80.9 us

profile of v6, /device:TPU:1, one launch (start us, length us, event | category | flops | bytes accessed | tf_op | source)
XLA Modules:
  0.0 81.5 jit_solution(14537068892149440997)
XLA Ops:
  0.0 80.9 %truncate.1 = f32[128,128]{1,0:T(8,128)S(1)} custom-call(f32[32,4,8,128]{3,2,1,0:T(8,128)} %bitcast.6, bf16[4,4,64,128]{3,2,1,0:T(8,128)(2,1)} %bitcast.7), custom_call_target="tpu_custom_call" | custom-call | tf_op jit(solution)/shard_map/truncate/pallas_call | solution.py:380
  80.9 0.6 copy.5

commit v7 on v6

--- a/solution.py
+++ b/solution.py
@@ -264,7 +264,6 @@
     after_core(0)
     after_core(3)
     after_core(1)
-    after_y(0)
     if chained:
         pl.semaphore_wait(far_sem, len(step_two))
     landed(flat.at[quarter(2), :], x_in.at[2])
@@ -278,6 +277,7 @@
         src = small.at[lax.rem(c + dc, nc), lax.rem(y + dy, ny), lax.rem(zl + dz, nzl)]
         copy(src, s_in.at[n + 1], si_in, device(dzl=dz, dc=dc, dy=dy))
     gram(2)
+    after_y(0)
     after_y(3)
     after_y(1)
     after_core(2)
@@ -295,63 +295,62 @@
 
     line = nzl * CHUNK
 
-    def place(dx, dy, core):
-        b = (lax.rem(x + dx, nx) * nzl + lax.rem(y + dy, ny)) * nc + core
-        return pl.ds(pl.multiple_of(b * line, line), line)
-
-    mine = place(0, 0, c)
-
     def hops(p):
         return min(p[0], nx - p[0]) + min(p[1], ny - p[1])
 
+    def group_of(p):
+        return min(p[0], nx - p[0])
+
     def gather_spread(k):
-        src = images.at[k, mine, :]
-        for p in sorted(plane, key=lambda p: -hops(p)):
-            copy(src, src, p_in.at[k, int(hops(p) > 2)], device(dx=p[0], dy=p[1]))
-        copy(src, src, q_in.at[k], device(dc=1))
-
-    def gather_pass(k, far):
-        group = [p for p in plane if (hops(p) > 2) == far]
-        landed(images.at[k, pl.ds(0, len(group) * line), :], p_in.at[k, int(far)])
-        for dx, dy in group:
-            src = images.at[k, place(nx - dx, ny - dy, c), :]
-            copy(src, src, q_in.at[k], device(dc=1))
+        src = images.at[k, x, y, c]
+        for p in sorted(plane, key=lambda p: (-group_of(p), -hops(p))):
+            copy(src, src, p_in.at[k, group_of(p)], device(dx=p[0], dy=p[1]))
+
+    def gather_pass(k, group):
+        like = (images.at[k, 0, 1:, 0], images.at[k, 0:2, :, 0], images.at[k, 0, :, 0])[group]
+        landed(like, p_in.at[k, group])
+        for dx in range(nx):
+            if group_of((dx, 0)) == group:
+                src = images.at[k, lax.rem(x + dx, nx), :, c]
+                copy(src, src, q_in.at[k], device(dc=1))
 
     def gather_end(k):
-        landed(images.at[k, pl.ds(0, nx * ny * line), :], q_in.at[k])
+        landed(images.at[k, :, :, 0], q_in.at[k])
 
     def factor(k0, k1):
         lax.fori_loop(k0, k1, lambda b, _: (panel_step(b, work, inverse), 0)[1], 0)
 
     landed(s_line.at[1:], sl_in)
-    images[0, mine, :] = sum(
+    images[0, x, y, c] = sum(
         s_line[q * nzl : (q + 1) * nzl] for q in range(nzh)
     ).reshape(line, RANK)
     gather_spread(0)
     after_zh(0)
     after_zh(3)
     after_zh(1)
-    gather_pass(0, False)
+    gather_pass(0, 0)
+    gather_pass(0, 1)
     after_zh(2)
-    gather_pass(0, True)
+    gather_pass(0, 2)
     gather_end(0)
-    image[...] = to_unit(images[0])
+    image[...] = to_unit(images[0].reshape(image.shape))
 
     def times(strip, d):
         return jnp.dot(strip, image[quarter(d), :], preferred_element_type=F32, precision=lax.Precision.HIGHEST)
 
     landed(own.at[:, 1:], o_in)
     for k in range(1, ITERS):
-        images[k, mine, :] = sum(times(own[d].reshape(line, wide), d) for d in range(nx))
+        images[k, x, y, c] = sum(times(own[d].reshape(line, wide), d) for d in range(nx))
         gather_spread(k)
         start_factor(image[...], work)
         factor(0, 5)
-        gather_pass(k, False)
+        gather_pass(k, 0)
+        gather_pass(k, 1)
         factor(5, RANK // PANEL)
-        gather_pass(k, True)
+        gather_pass(k, 2)
         gather_end(k)
         image[...] = to_unit(lax.dot_general(
-            images[k], inverse[...], (((1,), (1,)), ((), ())),
+            images[k].reshape(image.shape), inverse[...], (((1,), (1,)), ((), ())),
             preferred_element_type=F32, precision=lax.Precision.HIGHEST,
         ))
     start_factor(image[...], work)
@@ -399,12 +398,12 @@
             vmem((nc * ny * nzl, CHUNK, RANK), F32),
             vmem((nzh * nzl, CHUNK, RANK), F32),
             vmem((order, RANK), F32),
-            vmem((ITERS, order, RANK), F32),
+            vmem((ITERS, nx, ny, nc, nzl * CHUNK, RANK), F32),
             vmem((RANK, 2 * RANK), F32),
             vmem((RANK, RANK), F32),
             dma((nzl + nx + 1,)), dma(()),
             dma((nzl, nc)), dma((3,)), dma((nx,)), dma((nx,)), dma((nx,)), dma((nx,)),
-            dma(()), dma(()), dma(()), dma((ITERS, 2)), dma((ITERS,)),
+            dma(()), dma(()), dma(()), dma((ITERS, 3)), dma((ITERS,)),
             pltpu.SemaphoreType.REGULAR, pltpu.SemaphoreType.REGULAR,
         ],
         compiler_params=pltpu.CompilerParams(

time: 81.6 us -> 83 us (1.017)
  Pallas kernels: 80.9 us -> 82.2 us
    pallas_call x1, Pallas kernels: 80.9 us -> 82.2 us  [local(): pl.pallas_call(functools.partial(kernel, grid), out_shape=jax.ShapeDtypeS...]
where the time goes in v7:
time: 83 us; the launch traced here: 82.8 us
  Pallas kernels  82.2 us (99%)
    pallas_call x1, Pallas kernels, local(): pl.pallas_call(functools.partial(kernel, grid), out_shape=jax.ShapeDtypeS...  82.2 us

profile of v7, /device:TPU:1, one launch (start us, length us, event | category | flops | bytes accessed | tf_op | source)
XLA Modules:
  0.0 82.8 jit_solution(381586641740886726)
XLA Ops:
  0.0 82.2 %truncate.1 = f32[128,128]{1,0:T(8,128)S(1)} custom-call(f32[32,4,8,128]{3,2,1,0:T(8,128)} %bitcast.6, bf16[4,4,64,128]{3,2,1,0:T(8,128)(2,1)} %bitcast.7), custom_call_target="tpu_custom_call" | custom-call | tf_op jit(solution)/shard_map/truncate/pallas_call | solution.py:379
  82.2 0.6 copy.5

commit v8 on v7

--- a/solution.py
+++ b/solution.py
@@ -264,10 +264,12 @@
     after_core(0)
     after_core(3)
     after_core(1)
+    after_y(0)
     if chained:
         pl.semaphore_wait(far_sem, len(step_two))
     landed(flat.at[quarter(2), :], x_in.at[2])
 
+    gram(2)
     inner = inner + weigh(2)
     first_image = sum(against(tops, t) for t in thirds(inner)[::-1])
     small[...] = first_image.reshape(small.shape)
@@ -276,11 +278,9 @@
     for n, (dy, dz, dc) in sorted(enumerate(block_peers), key=lambda p: -reach(p[1])):
         src = small.at[lax.rem(c + dc, nc), lax.rem(y + dy, ny), lax.rem(zl + dz, nzl)]
         copy(src, s_in.at[n + 1], si_in, device(dzl=dz, dc=dc, dy=dy))
-    gram(2)
-    after_y(0)
+    after_core(2)
     after_y(3)
     after_y(1)
-    after_core(2)
     after_zl(0)
     after_y(2)
 
@@ -289,9 +289,9 @@
     s_line[place_z] = jnp.sum(s_in[...], axis=0)
     for d in sorted(line_of, key=lambda d: -min(d, nzl * nzh - d)):
         copy(s_line.at[place_z], s_line.at[place_z], sl_in, along_z(d))
+    after_zl(2)
     after_zl(3)
     after_zl(1)
-    after_zl(2)
 
     line = nzl * CHUNK
 

time: 83 us -> 80.9 us (0.975)
  Pallas kernels: 82.2 us -> 80.1 us
    pallas_call x1, Pallas kernels: 82.2 us -> 80.1 us  [local(): pl.pallas_call(functools.partial(kernel, grid), out_shape=jax.ShapeDtypeS...]
where the time goes in v8:
time: 80.9 us; the launch traced here: 80.8 us
  Pallas kernels  80.1 us (99%)
    pallas_call x1, Pallas kernels, local(): pl.pallas_call(functools.partial(kernel, grid), out_shape=jax.ShapeDtypeS...  80.1 us

profile of v8, /device:TPU:1, one launch (start us, length us, event | category | flops | bytes accessed | tf_op | source)
XLA Modules:
  0.0 80.8 jit_solution(12335911279837479656)
XLA Ops:
  0.0 80.1 %truncate.1 = f32[128,128]{1,0:T(8,128)S(1)} custom-call(f32[32,4,8,128]{3,2,1,0:T(8,128)} %bitcast.6, bf16[4,4,64,128]{3,2,1,0:T(8,128)(2,1)} %bitcast.7), custom_call_target="tpu_custom_call" | custom-call | tf_op jit(solution)/shard_map/truncate/pallas_call | solution.py:379
  80.2 0.6 copy.5

commit v9 on v8

--- a/solution.py
+++ b/solution.py
@@ -318,7 +318,8 @@
         landed(images.at[k, :, :, 0], q_in.at[k])
 
     def factor(k0, k1):
-        lax.fori_loop(k0, k1, lambda b, _: (panel_step(b, work, inverse), 0)[1], 0)
+        for b in range(k0, k1):
+            panel_step(b, work, inverse)
 
     landed(s_line.at[1:], sl_in)
     images[0, x, y, c] = sum(

time: 80.9 us -> 80.1 us (level)
    pallas_call x1, Pallas kernels: 80.1 us -> 79.3 us  [local(): pl.pallas_call(functools.partial(kernel, grid), out_shape=jax.ShapeDtypeS...]
where the time goes in v9:
time: 80.1 us; the launch traced here: 80 us
  Pallas kernels  79.3 us (99%)
    pallas_call x1, Pallas kernels, local(): pl.pallas_call(functools.partial(kernel, grid), out_shape=jax.ShapeDtypeS...  79.3 us

profile of v9, /device:TPU:1, one launch (start us, length us, event | category | flops | bytes accessed | tf_op | source)
XLA Modules:
  0.0 80.0 jit_solution(4566356133792051413)
XLA Ops:
  0.0 79.3 %truncate.1 = f32[128,128]{1,0:T(8,128)S(1)} custom-call(f32[32,4,8,128]{3,2,1,0:T(8,128)} %bitcast.6, bf16[4,4,64,128]{3,2,1,0:T(8,128)(2,1)} %bitcast.7), custom_call_target="tpu_custom_call" | custom-call | tf_op jit(solution)/shard_map/truncate/pallas_call | solution.py:380
  79.3 0.6 copy.5
